TPU v7x, 32 devices: a whole 2x2x4 slice. The times are simulated.
32 devices in a mesh: dp: 4 (over y, x), cp: 8 (over z, core).
Axes of the slice: x: 2, y: 2, z: 4, core: 2. Of those that a mesh axis runs over, the one named last changes fastest.
Arguments:
- tokens: bfloat16 [4096, 1536], P(('dp', 'cp')), may hold values from -6 to 6
- output_cotangent: bfloat16 [4096, 1536], P(('dp', 'cp')), may hold values from -6 to 6
- sequence_lengths: int32 [4, 4], P('dp'), may hold values from 1 to 512, as said below
- block_order: int32 [4, 8], P('dp'), may hold values from 0 to 7, as said below
- attn_input: float32 [1536, 2560], P(('dp', 'cp')), may hold values from -0.15625 to 0.15625
- input_moment: float32 [1536, 2560], P(('dp', 'cp')), may hold values from -40 to 40
- input_square: float32 [1536, 2560], P(('dp', 'cp')), may hold values from 217.088 to 860.16
- attn_output: float32 [1536, 1536], P(('dp', 'cp')), may hold values from -1.25 to 1.25
- output_moment: float32 [1536, 1536], P(('dp', 'cp')), may hold values from -5 to 5
- output_square: float32 [1536, 1536], P(('dp', 'cp')), may hold values from 3.36 to 13.6
- gate_up: float32 [1536, 13824], P(('dp', 'cp')), may hold values from -0.15625 to 0.15625
- gateup_moment: float32 [1536, 13824], P(('dp', 'cp')), may hold values from -8 to 8
- gateup_square: float32 [1536, 13824], P(('dp', 'cp')), may hold values from 8.6016 to 34.4064
- down_weight: float32 [6912, 1536], P(('dp', 'cp')), may hold values from -0.078125 to 0.078125
- down_moment: float32 [6912, 1536], P(('dp', 'cp')), may hold values from -20 to 20
- down_square: float32 [6912, 1536], P(('dp', 'cp')), may hold values from 53.248 to 217.088
- norm_gains: float32 [3200], replicated, may hold values from 0.5 to 1.5
- gains_moment: float32 [3200], replicated, may hold values from -40 to 40
- gains_square: float32 [3200], replicated, may hold values from 217.088 to 860.16
Outputs:
- mixed: bfloat16 [4096, 1536], P(('dp', 'cp'))
- token_gradient: float32 [4096, 1536], P(('dp', 'cp'))
- input_next: float32 [1536, 2560], P(('dp', 'cp'))
- input_moment_next: float32 [1536, 2560], P(('dp', 'cp'))
- input_square_next: float32 [1536, 2560], P(('dp', 'cp'))
- output_next: float32 [1536, 1536], P(('dp', 'cp'))
- output_moment_next: float32 [1536, 1536], P(('dp', 'cp'))
- output_square_next: float32 [1536, 1536], P(('dp', 'cp'))
- gateup_next: float32 [1536, 13824], P(('dp', 'cp'))
- gateup_moment_next: float32 [1536, 13824], P(('dp', 'cp'))
- gateup_square_next: float32 [1536, 13824], P(('dp', 'cp'))
- down_next: float32 [6912, 1536], P(('dp', 'cp'))
- down_moment_next: float32 [6912, 1536], P(('dp', 'cp'))
- down_square_next: float32 [6912, 1536], P(('dp', 'cp'))
- gains_next: float32 [3200], replicated
- gains_moment_next: float32 [3200], replicated
- gains_square_next: float32 [3200], replicated
Inputs may be any that keep to these rules, and one draw needn't show every extreme that they name: `sequence_lengths`: each row holds 4 lengths, packed in order into its group's 1024 positions and summing to 1024; the largest in each row is exactly 512. `block_order`: each row is a permutation of the 8 blocks of its group's packed tokens.
All inputs are finite; a program needn't handle non-finite values.
Results may differ from a plain program's by a relative error of at most 0.025.
Values may be sent and summed in bfloat16 or wider, within the bound.
A program may use at most 384 MiB of HBM per device.

v0:
```python
import functools
import math

import jax
import jax.numpy as jnp
from jax import lax
from jax.experimental import pallas as pl
from jax.experimental.pallas import tpu as pltpu
from jax.sharding import PartitionSpec as P

HEADS = 24
KV_HEADS = 8
HEAD_DIM = 64
FF = 6912
STEP = 10


norm_eps = 1e-05
rope_base = 1000000.0
beta_one = 0.9
beta_two = 0.95
adam_eps = 1e-08
rate_input = 0.06
rate_output = 0.9
rate_gateup = 0.06
rate_down = 0.03
rate_gains = 0.5
weight_decay = 0.1
masked_score = -1e30


def rope_tables(offsets):
    half_dim = HEAD_DIM // 2
    freqs = jnp.exp(
        jnp.arange(half_dim, dtype=jnp.float32) * (-2.0 * math.log(rope_base) / HEAD_DIM)
    )
    angles = offsets.astype(jnp.float32)[:, None] * freqs[None, :]
    return (jnp.cos(angles), jnp.sin(angles))


def rotate(values, cosine, sine):
    half_dim = HEAD_DIM // 2
    first_half = values[..., :half_dim]
    second_half = values[..., half_dim:]
    cos_wide = cosine[:, None, :]
    sin_wide = sine[:, None, :]
    return jnp.concatenate(
        [
            first_half * cos_wide - second_half * sin_wide,
            second_half * cos_wide + first_half * sin_wide,
        ],
        axis=-1,
    )


def locate(positions, lengths):
    seq_ends = jnp.cumsum(lengths)
    starts = seq_ends - lengths
    doc_index = jnp.sum((positions[:, None] >= seq_ends[None, :]).astype(jnp.int32), axis=1)
    picked = (doc_index[:, None] == jnp.arange(lengths.shape[0], dtype=jnp.int32)[None, :]).astype(
        jnp.int32
    )
    return (doc_index, positions - jnp.sum(picked * starts[None, :], axis=1))


def rms_parts(values):
    inverse = lax.rsqrt(jnp.mean(values * values, axis=-1, keepdims=True) + norm_eps)
    return (values * inverse, inverse)


def norm_back(d_normed, normal_hat, inverse):
    return inverse * (
        d_normed - normal_hat * jnp.mean(d_normed * normal_hat, axis=-1, keepdims=True)
    )


def contract_rows(left, right):
    return lax.dot_general(
        left, right, (((0,), (0,)), ((), ())), preferred_element_type=jnp.float32
    )


def contract_cols(left, right):
    return lax.dot_general(
        left, right, (((1,), (1,)), ((), ())), preferred_element_type=jnp.float32
    )


def owner_order(values, data_count, context_count):
    lead = values.shape[0]
    each = values.shape[1] // (data_count * context_count)
    return (
        values.reshape(lead, data_count, context_count, each)
        .transpose(0, 2, 1, 3)
        .reshape(lead, values.shape[1])
    )


def adam_update(weight, first_moment, second_moment, gradient, rate, decay):
    first_moment = beta_one * first_moment + (1.0 - beta_one) * gradient
    second_moment = beta_two * second_moment + (1.0 - beta_two) * gradient * gradient
    first_fix = 1.0 - beta_one**STEP
    second_fix = 1.0 - beta_two**STEP
    direction = first_moment / first_fix / (jnp.sqrt(second_moment / second_fix) + adam_eps)
    return (weight - rate * (direction + decay * weight), first_moment, second_moment)


def on_device(
    tokens,
    output_cotangent,
    sequence_lengths,
    block_order,
    attn_input,
    input_moment,
    input_square,
    attn_output,
    output_moment,
    output_square,
    gate_up,
    gateup_moment,
    gateup_square,
    down_weight,
    down_moment,
    down_square,
    norm_gains,
    gains_moment,
    gains_square,
):
    row_count = tokens.shape[0]
    model_width = tokens.shape[1]
    q_width = HEADS * HEAD_DIM
    kv_width = KV_HEADS * HEAD_DIM
    proj_width = q_width + 2 * kv_width
    head_groups = HEADS // KV_HEADS
    score_scale = HEAD_DIM ** (-0.5)
    gain_one = norm_gains[:model_width]
    gain_two = norm_gains[model_width : 2 * model_width]
    gain_query = norm_gains[2 * model_width : 2 * model_width + HEAD_DIM]
    gain_key = norm_gains[2 * model_width + HEAD_DIM :]
    seq_lens = sequence_lengths[0]
    order_row = block_order[0]
    context_count = lax.axis_size("cp")
    data_count = lax.axis_size("dp")
    own_slot = lax.axis_index("cp")
    offsets = jnp.arange(row_count, dtype=jnp.int32)
    own_block = jnp.sum(
        jnp.where(jnp.arange(context_count, dtype=jnp.int32) == own_slot, order_row, 0)
    )
    positions = own_block * row_count + offsets
    key_positions = (order_row[:, None] * row_count + offsets[None, :]).reshape(
        context_count * row_count
    )
    doc_index, seq_offset = locate(positions, seq_lens)
    key_doc = locate(key_positions, seq_lens)[0]
    cosine, sine = rope_tables(seq_offset)
    input_bf = attn_input.astype(jnp.bfloat16)
    output_bf = attn_output.astype(jnp.bfloat16)
    gateup_bf = gate_up.astype(jnp.bfloat16)
    down_bf = down_weight.astype(jnp.bfloat16)
    input_all, output_all = (
        lax.all_gather(input_bf, ("dp", "cp"), axis=0, tiled=True),
        lax.all_gather(output_bf, ("dp", "cp"), axis=0, tiled=True),
    )
    x_float = tokens.astype(jnp.float32)
    hat_one, inv_one = rms_parts(x_float)
    normed_one = (hat_one * gain_one).astype(jnp.bfloat16)
    projected = jnp.dot(normed_one, input_all, preferred_element_type=jnp.float32)
    query_raw = projected[:, :q_width].reshape(row_count, HEADS, HEAD_DIM)
    key_raw = projected[:, q_width : q_width + kv_width].reshape(row_count, KV_HEADS, HEAD_DIM)
    value_raw = projected[:, q_width + kv_width :]
    hat_query, inv_query = rms_parts(query_raw)
    hat_key, inv_key = rms_parts(key_raw)
    queries = rotate(hat_query * gain_query, cosine, sine).astype(jnp.bfloat16)
    key_rot = rotate(hat_key * gain_key, cosine, sine)
    key_value = jnp.concatenate([key_rot.reshape(row_count, kv_width), value_raw], axis=1).astype(
        jnp.bfloat16
    )
    kv_all = lax.all_gather(key_value, "cp", axis=0, tiled=True)
    total_keys = kv_all.shape[0]
    key_span = min(512, total_keys)
    block_count = total_keys // key_span
    kv_blocks = kv_all.reshape(block_count, key_span, 2 * kv_width)
    pos_blocks = key_positions.reshape(block_count, key_span)
    doc_blocks = key_doc.reshape(block_count, key_span)
    query_group = queries.reshape(row_count, KV_HEADS, head_groups, HEAD_DIM)

    def block_scores(kv_block, key_pos, key_docs):
        key_block = kv_block[:, :kv_width].reshape(key_span, KV_HEADS, HEAD_DIM)
        value_block = kv_block[:, kv_width:].reshape(key_span, KV_HEADS, HEAD_DIM)
        scores = (
            jnp.einsum("qhgd,khd->hgqk", query_group, key_block, preferred_element_type=jnp.float32)
            * score_scale
        )
        allowed = (doc_index[:, None] == key_docs[None, :]) & (
            key_pos[None, :] <= positions[:, None]
        )
        return (key_block, value_block, jnp.where(allowed, scores, masked_score), allowed)

    def forward_block(carry, items):
        run_max, run_total, run_sum = carry
        key_block, value_block, scores, allowed = block_scores(*items)
        new_max = jnp.maximum(run_max, jnp.max(scores, axis=-1))
        weights = jnp.where(allowed, jnp.exp(scores - new_max[..., None]), 0.0)
        factor = jnp.exp(run_max - new_max)
        run_total = run_total * factor + jnp.sum(weights, axis=-1)
        run_sum = run_sum * factor[..., None] + jnp.einsum(
            "hgqk,khd->hgqd",
            weights.astype(jnp.bfloat16),
            value_block,
            preferred_element_type=jnp.float32,
        )
        return ((new_max, run_total, run_sum), None)

    start_state = (
        jnp.full((KV_HEADS, head_groups, row_count), masked_score, jnp.float32),
        jnp.zeros((KV_HEADS, head_groups, row_count), jnp.float32),
        jnp.zeros((KV_HEADS, head_groups, row_count, HEAD_DIM), jnp.float32),
    )
    (run_max, run_total, run_sum), unused = lax.scan(
        forward_block, start_state, (kv_blocks, pos_blocks, doc_blocks)
    )
    attended = run_sum / run_total[..., None]
    log_total = run_max + jnp.log(run_total)
    attn_flat = attended.transpose(2, 0, 1, 3).reshape(row_count, q_width).astype(jnp.bfloat16)
    residual = x_float + jnp.dot(attn_flat, output_all, preferred_element_type=jnp.float32)
    hat_two, inv_two = rms_parts(residual)
    normed_two = (hat_two * gain_two).astype(jnp.bfloat16)
    columns = normed_two
    gate_both = jnp.dot(
        columns,
        lax.all_gather(gateup_bf, ("dp", "cp"), axis=0, tiled=True),
        preferred_element_type=jnp.float32,
    )
    gate_part = gate_both[:, :FF]
    up_part = gate_both[:, FF:]
    gate_sig = jax.nn.sigmoid(gate_part)
    gate_act = gate_part * gate_sig
    hidden = (gate_act * up_part).astype(jnp.bfloat16)
    columns = hidden
    ff_result = jnp.dot(
        columns,
        lax.all_gather(down_bf, ("dp", "cp"), axis=0, tiled=True),
        preferred_element_type=jnp.float32,
    )
    mixed = (residual + ff_result).astype(jnp.bfloat16)
    d_hidden = contract_cols(
        output_cotangent, lax.all_gather(down_bf, ("dp", "cp"), axis=0, tiled=True)
    )
    d_gate = d_hidden * up_part * (gate_sig * (1.0 + gate_part * (1.0 - gate_sig)))
    d_up = d_hidden * gate_act
    d_gate_both = jnp.concatenate([d_gate, d_up], axis=1).astype(jnp.bfloat16)
    d_normed_two = contract_cols(
        d_gate_both, lax.all_gather(gateup_bf, ("dp", "cp"), axis=0, tiled=True)
    )
    grad_gain_two = jnp.sum(d_normed_two * hat_two, axis=0)
    d_residual = output_cotangent.astype(jnp.float32) + norm_back(
        d_normed_two * gain_two, hat_two, inv_two
    )
    d_branch = d_residual.astype(jnp.bfloat16)
    input_back, output_back = (input_all, output_all)
    d_flat = contract_cols(d_branch, output_back).astype(jnp.bfloat16)
    d_attended = d_flat.reshape(row_count, KV_HEADS, head_groups, HEAD_DIM).transpose(1, 2, 0, 3)
    delta = jnp.sum(d_attended.astype(jnp.float32) * attended, axis=-1)

    def backward_block(d_query_sum, items):
        key_block, value_block, scores, allowed = block_scores(*items)
        probs = jnp.where(allowed, jnp.exp(scores - log_total[..., None]), 0.0)
        d_probs = jnp.einsum(
            "hgqd,khd->hgqk", d_attended, value_block, preferred_element_type=jnp.float32
        )
        d_scores = (probs * (d_probs - delta[..., None])).astype(jnp.bfloat16)
        d_query_sum = (
            d_query_sum
            + jnp.einsum("hgqk,khd->hgqd", d_scores, key_block, preferred_element_type=jnp.float32)
            * score_scale
        )
        d_keys = (
            jnp.einsum("hgqk,qhgd->khd", d_scores, query_group, preferred_element_type=jnp.float32)
            * score_scale
        )
        d_values = jnp.einsum(
            "hgqk,hgqd->khd",
            probs.astype(jnp.bfloat16),
            d_attended,
            preferred_element_type=jnp.float32,
        )
        return (
            d_query_sum,
            jnp.concatenate(
                [d_keys.reshape(key_span, kv_width), d_values.reshape(key_span, kv_width)], axis=1
            ),
        )

    d_query_sum, d_kv_blocks = lax.scan(
        backward_block,
        jnp.zeros((KV_HEADS, head_groups, row_count, HEAD_DIM), jnp.float32),
        (kv_blocks, pos_blocks, doc_blocks),
    )
    d_kv = lax.psum_scatter(
        d_kv_blocks.reshape(total_keys, 2 * kv_width).astype(jnp.bfloat16),
        "cp",
        scatter_dimension=0,
        tiled=True,
    ).astype(jnp.float32)
    d_query_rot = rotate(
        d_query_sum.transpose(2, 0, 1, 3).reshape(row_count, HEADS, HEAD_DIM), cosine, -sine
    )
    grad_gain_query = jnp.sum(d_query_rot * hat_query, axis=(0, 1))
    d_query_raw = norm_back(d_query_rot * gain_query, hat_query, inv_query)
    d_key_rot = rotate(d_kv[:, :kv_width].reshape(row_count, KV_HEADS, HEAD_DIM), cosine, -sine)
    grad_gain_key = jnp.sum(d_key_rot * hat_key, axis=(0, 1))
    d_key_raw = norm_back(d_key_rot * gain_key, hat_key, inv_key)
    d_projected = jnp.concatenate(
        [
            d_query_raw.reshape(row_count, q_width),
            d_key_raw.reshape(row_count, kv_width),
            d_kv[:, kv_width:],
        ],
        axis=1,
    ).astype(jnp.bfloat16)
    d_normed_one = contract_cols(d_projected, input_back)
    grad_gain_one = jnp.sum(d_normed_one * hat_one, axis=0)
    token_gradient = d_residual + norm_back(d_normed_one * gain_one, hat_one, inv_one)

    def make_wide(first_src, attn_src, second_src):

        def wide_terms(row_start, row_total):
            return jnp.concatenate(
                [
                    contract_rows(first_src, d_projected),
                    contract_rows(attn_src, d_branch),
                    contract_rows(second_src, d_gate_both),
                ],
                axis=1,
            )

        return wide_terms

    def make_down(hidden_src):

        def down_terms(row_start, row_total):
            return contract_rows(hidden_src, output_cotangent)

        return down_terms

    shard_rows = attn_input.shape[0]
    down_rows = down_weight.shape[0]
    wide_fn = make_wide(
        owner_order(normed_one, data_count, context_count),
        owner_order(attn_flat, data_count, context_count),
        owner_order(normed_two, data_count, context_count),
    )
    down_fn = make_down(owner_order(hidden, data_count, context_count))
    group_wide = lax.psum_scatter(
        wide_fn(jnp.int32(0), lax.axis_size("cp") * (shard_rows * data_count)).astype(jnp.bfloat16),
        "cp",
        scatter_dimension=0,
        tiled=True,
    )
    group_down = lax.psum_scatter(
        down_fn(jnp.int32(0), lax.axis_size("cp") * (down_rows * data_count)).astype(jnp.bfloat16),
        "cp",
        scatter_dimension=0,
        tiled=True,
    )
    wide_grads, down_grads = (
        lax.psum_scatter(group_wide, "dp", scatter_dimension=0, tiled=True).astype(jnp.float32),
        lax.psum_scatter(group_down, "dp", scatter_dimension=0, tiled=True).astype(jnp.float32),
    )
    gain_grads = lax.psum(
        jnp.concatenate([grad_gain_one, grad_gain_two, grad_gain_query, grad_gain_key]),
        ("dp", "cp"),
    )
    grad_input = wide_grads[:, :proj_width]
    grad_output = wide_grads[:, proj_width : proj_width + model_width]
    grad_gateup = wide_grads[:, proj_width + model_width :]
    input_next, input_moment_next, input_square_next = adam_update(
        attn_input, input_moment, input_square, grad_input, rate_input, weight_decay
    )
    output_next, output_moment_next, output_square_next = adam_update(
        attn_output, output_moment, output_square, grad_output, rate_output, weight_decay
    )
    gateup_next, gateup_moment_next, gateup_square_next = adam_update(
        gate_up, gateup_moment, gateup_square, grad_gateup, rate_gateup, weight_decay
    )
    down_next, down_moment_next, down_square_next = adam_update(
        down_weight, down_moment, down_square, down_grads, rate_down, weight_decay
    )
    gains_next, gains_moment_next, gains_square_next = adam_update(
        norm_gains, gains_moment, gains_square, gain_grads, rate_gains, 0.0
    )
    return (
        mixed,
        token_gradient,
        input_next,
        input_moment_next,
        input_square_next,
        output_next,
        output_moment_next,
        output_square_next,
        gateup_next,
        gateup_moment_next,
        gateup_square_next,
        down_next,
        down_moment_next,
        down_square_next,
        gains_next,
        gains_moment_next,
        gains_square_next,
    )


MESH = pl.DeviceIdType.MESH


def place():
    dp = lax.axis_index("dp")
    cp = lax.axis_index("cp")
    return dp, cp, cp // 2, cp % 2


def greet(targets):
    barrier = pltpu.get_barrier_semaphore()
    for target in targets:
        pl.semaphore_signal(barrier, inc=1, device_id=target, device_id_type=MESH)
    pl.semaphore_wait(barrier, len(targets))


def send(source, target, send_sem, recv_sem, device):
    return pltpu.make_async_remote_copy(
        src_ref=source,
        dst_ref=target,
        send_sem=send_sem,
        recv_sem=recv_sem,
        device_id=device,
        device_id_type=MESH,
    )


class LineGather:
    def __init__(self, own_ref, all_ref, sems, where, depth, both=True):
        self.own, self.where, self.depth, self.both = own_ref, where, depth, both
        self.slot = all_ref if callable(all_ref) else lambda slot: all_ref.at[slot]
        self.right, self.left, self.sib, self.recv, self.local = sems

    @staticmethod
    def scratch(depth):
        return [pltpu.SemaphoreType.DMA((2 * depth,))] * 4 + [pltpu.SemaphoreType.DMA]

    def copy(self, kind, slot, source):
        dp, cp, z, core = self.where
        device = {"right": (dp, cp + 2), "left": (dp, cp - 2), "sib": (dp, cp ^ 1)}[kind]
        sem = {"right": self.right, "left": self.left, "sib": self.sib}[kind]
        return send(source, self.slot(slot), sem.at[slot], self.recv.at[slot], device)

    def keep(self):
        return pltpu.make_async_copy(self.own, self.slot(self.where[1]), self.local)

    def start(self):
        dp, cp, z, core = self.where

        @pl.when(z < self.depth - 1)
        def _():
            self.copy("right", cp, self.own).start()

        @pl.when(z > 0)
        def _():
            self.copy("left", cp, self.own).start()

        if self.both:
            self.copy("sib", cp, self.own).start()
        self.keep().start()

    def step(self, far):
        dp, cp, z, core = self.where

        @pl.when(z >= far)
        def _():
            slot = cp - 2 * far
            self.copy("right", slot, self.own).wait_recv()

            @pl.when(z < self.depth - 1)
            def _():
                self.copy("right", slot, self.slot(slot)).start()

            if self.both:
                self.copy("sib", slot, self.slot(slot)).start()

        @pl.when(z + far < self.depth)
        def _():
            slot = cp + 2 * far
            self.copy("left", slot, self.own).wait_recv()

            @pl.when(z > 0)
            def _():
                self.copy("left", slot, self.slot(slot)).start()

            if self.both:
                self.copy("sib", slot, self.slot(slot)).start()

    def arrive(self, spot):
        self.copy("sib", 1 - self.where[3] + 2 * spot, self.own).wait_recv()

    def finish(self, arrived=False):
        dp, cp, z, core = self.where
        if self.both and not arrived:
            for spot in range(self.depth):
                self.arrive(spot)
        if not arrived:
            self.keep().wait()
        for spot in range(self.depth):
            slot = 2 * spot + core
            if self.both:
                self.copy("sib", slot, self.own).wait_send()

            @pl.when((spot <= z) & (z < self.depth - 1))
            def _():
                self.copy("right", slot, self.own).wait_send()

            @pl.when((spot >= z) & (z > 0))
            def _():
                self.copy("left", slot, self.own).wait_send()


class Swap:
    def __init__(self, source_ref, target_ref, sems, where, count):
        self.source, self.where, self.count = source_ref, where, count
        self.slot = target_ref if callable(target_ref) else lambda slot: target_ref.at[slot]
        self.origin = source_ref if callable(source_ref) else lambda slot: source_ref.at[slot]
        self.sent, self.recv, self.local = sems

    @staticmethod
    def scratch(count):
        return [pltpu.SemaphoreType.DMA((count,))] * 2 + [pltpu.SemaphoreType.DMA]

    def copy(self, peer):
        dp, cp, z, core = self.where
        return send(
            self.origin(peer),
            self.slot(cp),
            self.sent.at[peer],
            self.recv.at[cp],
            (dp, peer),
        )

    def keep(self):
        cp = self.where[1]
        return pltpu.make_async_copy(self.origin(cp), self.slot(cp), self.local)

    def start(self):
        cp = self.where[1]
        for turn in range(self.count - 1, 0, -1):
            self.copy(cp ^ turn).start()
        self.keep().start()

    def arrive(self, peer):
        dp, cp, z, core = self.where
        send(
            self.origin(peer),
            self.slot(peer),
            self.sent.at[peer],
            self.recv.at[peer],
            (dp, peer),
        ).wait_recv()

    def finish_recv(self):
        cp = self.where[1]
        for turn in range(1, self.count):
            self.arrive(cp ^ turn)
        self.keep().wait()

    def finish_send(self):
        cp = self.where[1]
        for turn in range(1, self.count):
            self.copy(cp ^ turn).wait_send()


class RingSpread:
    def __init__(self, block, half, sems, where):
        self.block, self.half, self.where = block, half, where
        self.sent, self.recv = sems

    @staticmethod
    def scratch():
        return [pltpu.SemaphoreType.DMA((4,))] * 2

    def copy(self, kind, mine):
        dp, cp, z, core = self.where
        turn = (1, 2, 2, 1)[kind]
        if kind < 2:
            part = self.block(dp if mine else dp ^ turn)
        else:
            part = self.half(dp ^ (3 - turn) if mine else dp ^ 3, kind - 2)
        return send(part, part, self.sent.at[kind], self.recv.at[kind], (dp ^ turn, cp))

    def start(self):
        self.copy(0, True).start()
        self.copy(1, True).start()

    def forward(self):
        self.copy(0, False).wait_recv()
        self.copy(2, True).start()
        self.copy(1, False).wait_recv()
        self.copy(3, True).start()

    def finish(self):
        self.copy(2, False).wait_recv()
        self.copy(3, False).wait_recv()
        for kind in range(4):
            self.copy(kind, True).wait_send()


def turn_heads(values, cosine, sine):
    half = values.shape[0] // 2
    first, second = values[:half], values[half:]
    return jnp.concatenate([first * cosine - second * sine, second * cosine + first * sine], axis=0)


def head_hat(values):
    inverse = lax.rsqrt(jnp.mean(values * values, axis=0, keepdims=True) + norm_eps)
    return values * inverse, inverse


def lay_places(order_ref, lengths_ref, rows, count):
    spots = [order_ref[0, index] * rows for index in range(count)]
    lanes = lax.broadcasted_iota(jnp.int32, (1, rows), 1)
    lines = lax.broadcasted_iota(jnp.int32, (rows, 1), 0)
    place_row = jnp.concatenate([spot + lanes for spot in spots], axis=1)
    place_column = jnp.concatenate([spot + lines for spot in spots], axis=0)
    starts = jnp.zeros_like(place_row)
    begin = jnp.int32(0)
    for index in range(lengths_ref.shape[1] - 1):
        begin = begin + lengths_ref[0, index]
        starts = jnp.where(place_row >= begin, begin, starts)
    return place_row, place_column, starts


def to_column(row):
    size = row.shape[1]
    down = lax.broadcasted_iota(jnp.int32, (size, size), 0)
    across = lax.broadcasted_iota(jnp.int32, (size, size), 1)
    return jnp.sum(jnp.where(down == across, row, 0.0), axis=1, keepdims=True)


def split_gains(gains_ref, width):
    gain_one = gains_ref[:, :width]
    gain_two = gains_ref[:, width : 2 * width]
    gain_query = to_column(gains_ref[:, 2 * width : 2 * width + HEAD_DIM])
    gain_key = to_column(gains_ref[:, 2 * width + HEAD_DIM :])
    return gain_one, gain_two, gain_query, gain_key


def score_block(keys, queries, key_place, query_place, query_start):
    scores = jnp.dot(keys, queries, preferred_element_type=jnp.float32) * HEAD_DIM ** (-0.5)
    allowed = (key_place <= query_place) & (key_place >= query_start)
    return jnp.where(allowed, scores, masked_score), allowed


def front_kernel(
    tile,
    tokens_ref,
    gains_ref,
    order_ref,
    lengths_ref,
    input_ref,
    output_ref,
    gateup_ref,
    cotangent_own,
    normed_one_out,
    own_two,
    cotangent_all,
    input_out,
    output_out,
    gateup_out,
    raw_out,
    flat_out,
    total_out,
    residual_out,
    cosine_ref,
    sine_ref,
    input_send,
    output_own,
    gate_send,
    up_send,
    key_place_ref,
    query_place_ref,
    query_start_ref,
    normed_one,
    own_one,
    inputs,
    outputs,
    raw,
    queries,
    keys_up,
    values,
    flat_send,
    flat_recv,
    out_sems,
    *sems,
):
    where = place()
    dp, cp, z, core = where
    context_count = normed_one.shape[0]
    depth = context_count // 2
    rows = tokens_ref.shape[0]
    width = tokens_ref.shape[1]
    q_each = HEADS // KV_HEADS * HEAD_DIM
    take = iter(range(len(sems)))

    def some(count):
        return [sems[next(take)] for _ in range(count)]

    kv_each = HEAD_DIM
    for head in range(context_count):
        for start, begin, size in (
            (head * q_each, 0, q_each),
            (HEADS * HEAD_DIM + head * kv_each, q_each, kv_each),
            ((HEADS + KV_HEADS) * HEAD_DIM + head * kv_each, q_each + kv_each, kv_each),
        ):
            input_send[head, :, begin : begin + size] = input_ref[:, start : start + size].astype(
                jnp.bfloat16
            )
    hidden = gate_send.shape[2]
    piece = hidden // inputs.shape[0]
    half_width = gateup_ref.shape[1] // 2

    def cut_columns(target, base):
        for head in range(context_count):
            target[head] = jnp.concatenate(
                [
                    gateup_ref[:, pl.ds(base + (group * context_count + head) * piece, piece)]
                    for group in range(inputs.shape[0])
                ],
                axis=1,
            ).astype(jnp.bfloat16)

    cut_columns(gate_send, 0)
    greet([(dp, cp ^ turn) for turn in range(1, context_count)] + [(dp ^ 1, cp), (dp ^ 2, cp)])
    token_line = LineGather(own_one, normed_one, some(5), where, depth)
    cotangent_line = LineGather(cotangent_own, cotangent_all, some(5), where, depth)
    output_line = LineGather(
        output_own, lambda slot: outputs.at[dp, slot // 2, core], some(5), where, depth, False
    )
    input_swap = Swap(input_send, inputs.at[dp], some(3), where, context_count)
    shard = input_send.shape[1]

    def gateup_slot(index):
        return lambda slot: gateup_out.at[index, dp, pl.ds(pl.multiple_of(slot * shard, 16), shard)]

    gate_swap = Swap(gate_send, gateup_slot(0), some(3), where, context_count)
    up_swap = Swap(up_send, gateup_slot(1), some(3), where, context_count)
    flat_swap = Swap(flat_send, flat_recv, some(3), where, context_count)
    input_ring = RingSpread(
        lambda d: inputs.at[d],
        lambda d, h: inputs.at[d, pl.ds(h * (context_count // 2), context_count // 2)],
        some(2),
        where,
    )
    output_ring = RingSpread(
        lambda d: outputs.at[d, :, core],
        lambda d, h: outputs.at[d, pl.ds(h * (depth // 2), depth // 2), core],
        some(2),
        where,
    )
    half_rows = gateup_out.shape[2] // 2

    def gateup_ring(index):
        return RingSpread(
            lambda d: gateup_out.at[index, d],
            lambda d, h: gateup_out.at[index, d, pl.ds(h * half_rows, half_rows)],
            some(2),
            where,
        )

    gate_ring, up_ring = gateup_ring(0), gateup_ring(1)
    share_sent, share_recv = some(2)

    def share(mine):
        part = outputs.at[:, :, core if mine else 1 - core]
        return send(part, part, share_sent, share_recv, (dp, cp ^ 1))

    input_swap.start()
    gate_swap.start()
    gain_one, gain_two, gain_query, gain_key = split_gains(gains_ref, width)
    x_float = tokens_ref[...].astype(jnp.float32)
    hat_one, _ = rms_parts(x_float)
    own_one[...] = (hat_one * gain_one).astype(jnp.bfloat16)
    output_own[...] = output_ref[...].astype(jnp.bfloat16)
    cut_columns(up_send, half_width)
    place_row, place_column, starts = lay_places(order_ref, lengths_ref, rows, context_count)
    query_place_ref[...] = place_row
    key_place_ref[...] = place_column
    query_start_ref[...] = starts
    pair_index = lax.broadcasted_iota(jnp.int32, (HEAD_DIM // 2, 1), 0).astype(jnp.float32)
    angles = (place_row - starts).astype(jnp.float32) * jnp.exp(
        pair_index * (-2.0 * math.log(rope_base) / HEAD_DIM)
    )
    cosine_ref[...] = jnp.cos(angles)
    sine_ref[...] = jnp.sin(angles)
    input_swap.finish_recv()
    input_ring.start()
    gate_swap.finish_recv()
    gate_ring.start()
    up_swap.start()
    input_ring.forward()
    token_line.start()
    token_line.step(1)
    up_swap.finish_recv()
    up_ring.start()
    token_line.step(2)
    gate_ring.forward()
    output_line.start()
    token_line.step(3)
    token_line.finish()
    input_ring.finish()
    one_copy = pltpu.make_async_copy(normed_one, normed_one_out, out_sems.at[0])
    one_copy.start()
    input_copy = pltpu.make_async_copy(inputs, input_out, out_sems.at[1])
    input_copy.start()

    weights = inputs[...].reshape(width, inputs.shape[-1])

    def project(turn, carry):
        lanes = pl.ds(pl.multiple_of(turn * tile, tile), tile)
        block = normed_one[pl.ds(turn * (tile // rows), tile // rows)].reshape(tile, width)
        part = jnp.dot(block, weights, preferred_element_type=jnp.float32).T
        raw[:, lanes] = part
        cosine, sine = cosine_ref[:, lanes], sine_ref[:, lanes]
        for head in range(HEADS // KV_HEADS):
            hat, _ = head_hat(part[head * HEAD_DIM : (head + 1) * HEAD_DIM])
            queries[head * HEAD_DIM : (head + 1) * HEAD_DIM, lanes] = turn_heads(
                hat * gain_query, cosine, sine
            ).astype(jnp.bfloat16)
        hat, _ = head_hat(part[q_each : q_each + HEAD_DIM])
        key = turn_heads(hat * gain_key, cosine, sine)
        keys_up[pl.ds(pl.multiple_of(turn * tile, tile), tile)] = key.T.astype(jnp.bfloat16)
        values[:, lanes] = part[q_each + HEAD_DIM :].astype(jnp.bfloat16)
        return carry

    lax.fori_loop(0, normed_one.shape[0] * rows // tile, project, 0)
    raw_copy = pltpu.make_async_copy(raw, raw_out, out_sems.at[2])
    raw_copy.start()

    def attend(turn, carry):
        lanes = pl.ds(pl.multiple_of(turn * tile, tile), tile)
        query_place, query_start = query_place_ref[:, lanes], query_start_ref[:, lanes]

        @pl.when(turn == 0)
        def _():
            output_line.step(1)

        @pl.when(turn == 1)
        def _():
            output_line.step(2)
            output_line.step(3)

        @pl.when(turn == 2)
        def _():
            output_line.finish()
            output_ring.start()

        @pl.when(turn == 3)
        def _():
            cotangent_line.start()

        for head in range(HEADS // KV_HEADS):
            spot = pl.ds(head * HEAD_DIM, HEAD_DIM)
            scores, allowed = score_block(
                keys_up[...], queries[spot, lanes], key_place_ref[...], query_place, query_start
            )
            top = jnp.max(scores, axis=0, keepdims=True)
            exps = jnp.exp(scores - top)
            total = jnp.sum(exps, axis=0, keepdims=True)
            total_out[pl.ds(head, 1), lanes] = top + jnp.log(total)
            probs = (exps * (1.0 / total)).astype(jnp.bfloat16)
            attended = jnp.dot(values[...], probs, preferred_element_type=jnp.float32)
            for part in range(tile // rows):
                flat_send[turn * (tile // rows) + part, spot] = attended[
                    :, part * rows : (part + 1) * rows
                ].astype(jnp.bfloat16)
        return carry

    lax.fori_loop(0, depth, attend, 0)
    flat_swap.start()
    output_ring.forward()
    cotangent_line.step(1)
    output_ring.finish()
    share(True).start()
    share(False).wait_recv()
    output_copy = pltpu.make_async_copy(outputs, output_out, out_sems.at[3])
    output_copy.start()
    flat_swap.finish_recv()
    flat_copy = pltpu.make_async_copy(flat_recv, flat_out, out_sems.at[4])
    flat_copy.start()
    flat = flat_recv[...].reshape(HEADS * HEAD_DIM, rows).astype(jnp.float32).T.astype(jnp.bfloat16)
    residual = x_float + jnp.dot(
        flat, outputs[...].reshape(HEADS * HEAD_DIM, width), preferred_element_type=jnp.float32
    )
    residual_out[...] = residual
    hat_two, _ = rms_parts(residual)
    own_two[...] = (hat_two * gain_two).astype(jnp.bfloat16)
    cotangent_line.step(2)
    up_ring.forward()
    cotangent_line.step(3)
    cotangent_line.finish()
    gate_ring.finish()
    up_ring.finish()
    share(True).wait_send()
    for swap in (input_swap, gate_swap, up_swap, flat_swap):
        swap.finish_send()
    for copy in (one_copy, input_copy, raw_copy, output_copy, flat_copy):
        copy.wait()


def front(
    tokens,
    gains,
    order,
    lengths,
    attn_input,
    attn_output,
    gate_up,
    cotangent,
    data_count,
    context_count,
):
    rows, width = tokens.shape
    depth = context_count // 2
    group_rows = rows * context_count
    shard = attn_input.shape[0]
    each = attn_input.shape[1] // context_count
    hidden = gate_up.shape[1] // 2 // context_count
    q_each = HEADS // KV_HEADS * HEAD_DIM
    flat_width = HEADS * HEAD_DIM
    bf = jnp.bfloat16
    any_space = pl.BlockSpec(memory_space=pl.ANY)
    in_vmem = pl.BlockSpec(memory_space=pltpu.VMEM)
    in_smem = pl.BlockSpec(memory_space=pltpu.SMEM)
    shapes = [
        ((context_count, rows, width), bf, any_space),
        ((rows, width), bf, in_vmem),
        ((context_count, rows, width), bf, any_space),
        ((data_count, context_count, shard, each), bf, any_space),
        ((data_count, depth, 2, shard, width), bf, any_space),
        ((2, data_count, context_count * shard, hidden), bf, any_space),
        ((each, group_rows), jnp.float32, any_space),
        ((context_count, q_each, rows), bf, any_space),
        ((HEADS // KV_HEADS, group_rows), jnp.float32, in_vmem),
        ((rows, width), jnp.float32, in_vmem),
        ((HEAD_DIM // 2, group_rows), jnp.float32, in_vmem),
        ((HEAD_DIM // 2, group_rows), jnp.float32, in_vmem),
    ]
    return pl.pallas_call(
        functools.partial(front_kernel, 2 * rows),
        out_shape=[jax.ShapeDtypeStruct(shape, kind) for shape, kind, _ in shapes],
        in_specs=[in_vmem] * 2 + [in_smem] * 2 + [in_vmem] * 3 + [any_space],
        out_specs=[space for _, _, space in shapes],
        scratch_shapes=[
            pltpu.VMEM((context_count, shard, each), bf),
            pltpu.VMEM((shard, width), bf),
            pltpu.VMEM((context_count, shard, hidden), bf),
            pltpu.VMEM((context_count, shard, hidden), bf),
            pltpu.VMEM((group_rows, 1), jnp.int32),
            pltpu.VMEM((1, group_rows), jnp.int32),
            pltpu.VMEM((1, group_rows), jnp.int32),
            pltpu.VMEM((context_count, rows, width), bf),
            pltpu.VMEM((rows, width), bf),
            pltpu.VMEM((data_count, context_count, shard, each), bf),
            pltpu.VMEM((data_count, depth, 2, shard, width), bf),
            pltpu.VMEM((each, group_rows), jnp.float32),
            pltpu.VMEM((q_each, group_rows), bf),
            pltpu.VMEM((group_rows, HEAD_DIM), bf),
            pltpu.VMEM((HEAD_DIM, group_rows), bf),
            pltpu.VMEM((context_count, q_each, rows), bf),
            pltpu.VMEM((context_count, q_each, rows), bf),
            pltpu.SemaphoreType.DMA((6,)),
        ]
        + LineGather.scratch(depth) * 3
        + Swap.scratch(context_count) * 4
        + RingSpread.scratch() * 4
        + [pltpu.SemaphoreType.DMA] * 2,
        compiler_params=pltpu.CompilerParams(
            collective_id=0, has_side_effects=True, vmem_limit_bytes=56 * 2**20
        ),
        name="front",
    )(tokens, gains, order, lengths, attn_input, attn_output, gate_up, cotangent)


class LineScatter:
    cuts = 2

    def __init__(self, part_ref, out_ref, scratch, where, depth):
        self.part, self.out, self.where, self.depth = part_ref, out_ref, where, depth
        self.sib, self.line = scratch[:2]
        (
            self.sib_sent,
            self.sib_recv,
            self.right_sent,
            self.right_recv,
            self.left_sent,
            self.left_recv,
        ) = scratch[2:]
        self.size = part_ref.shape[1] // self.cuts

    @classmethod
    def scratch(cls, depth, rows, width):
        return [
            pltpu.VMEM((depth, rows, width), jnp.bfloat16),
            pltpu.VMEM((depth + 1, rows, width), jnp.bfloat16),
        ] + [pltpu.SemaphoreType.DMA((depth,))] * 2 + [
            pltpu.SemaphoreType.DMA((depth * cls.cuts,))
        ] * 4

    def pair(self, spot):
        dp, cp, z, core = self.where
        return send(
            self.part.at[2 * spot + 1 - core],
            self.sib.at[spot],
            self.sib_sent.at[spot],
            self.sib_recv.at[spot],
            (dp, cp ^ 1),
        )

    def rows(self, cut):
        return pl.ds(cut * self.size, self.size)

    def hop_right(self, spot, cut):
        dp, cp, z, core = self.where
        index = spot * self.cuts + cut
        return send(
            self.part.at[2 * spot + core, self.rows(cut)],
            self.line.at[spot + 1, self.rows(cut)],
            self.right_sent.at[index],
            self.right_recv.at[index],
            (dp, cp + 2),
        )

    def hop_left(self, spot, cut):
        dp, cp, z, core = self.where
        index = spot * self.cuts + cut
        return send(
            self.part.at[2 * spot + core, self.rows(cut)],
            self.line.at[spot, self.rows(cut)],
            self.left_sent.at[index],
            self.left_recv.at[index],
            (dp, cp - 2),
        )

    def order(self):
        spots = []
        for turn in range(self.depth):
            spots += [self.depth - 1 - turn, turn]
        return list(dict.fromkeys(spots))

    def chip_sum(self, spot, cut):
        rows = self.rows(cut)
        mine = self.part[2 * spot + self.where[3], rows].astype(jnp.float32)
        return mine + self.sib[spot, rows].astype(jnp.float32)

    def pass_on(self, spot, cut, arrived, slot, hop):
        total = self.chip_sum(spot, cut)
        if arrived is not None:
            arrived.wait_recv()
            total = total + self.line[slot, self.rows(cut)].astype(jnp.float32)
        self.part[2 * spot + self.where[3], self.rows(cut)] = total.astype(jnp.bfloat16)
        hop.start()

    def forward(self, spot, cuts=None):
        z, core = self.where[2], self.where[3]
        cuts = range(self.cuts) if cuts is None else cuts
        if 0 in cuts:

            @pl.when(z != spot)
            def _():
                self.pair(spot).wait_recv()

        for cut in cuts:
            right, left = self.hop_right(spot, cut), self.hop_left(spot, cut)

            @pl.when((z < spot) & (z > 0))
            def _():
                self.pass_on(spot, cut, right, spot + 1, right)

            @pl.when((z < spot) & (z == 0))
            def _():
                self.pass_on(spot, cut, None, None, right)

            @pl.when((z > spot) & (z < self.depth - 1))
            def _():
                self.pass_on(spot, cut, left, spot, left)

            @pl.when((z > spot) & (z == self.depth - 1))
            def _():
                self.pass_on(spot, cut, None, None, left)

    def finish(self):
        z = self.where[2]
        self.pair(z).wait_recv()
        for cut in range(self.cuts):
            rows = self.rows(cut)
            self.out[rows] = self.chip_sum(z, cut)

            @pl.when(z > 0)
            def _():
                self.hop_right(z, cut).wait_recv()
                self.out[rows] += self.line[z + 1, rows].astype(jnp.float32)

            @pl.when(z < self.depth - 1)
            def _():
                self.hop_left(z, cut).wait_recv()
                self.out[rows] += self.line[z, rows].astype(jnp.float32)

        for spot in range(self.depth):
            self.pair(spot).wait_send()

            @pl.when(z < spot)
            def _():
                for cut in range(self.cuts):
                    self.hop_right(spot, cut).wait_send()

            @pl.when(z > spot)
            def _():
                for cut in range(self.cuts):
                    self.hop_left(spot, cut).wait_send()


class RingReduce:
    def __init__(self, part, work, scratch, where):
        self.part, self.work, self.where = part, work, where
        self.from_x, self.from_y, self.x_sent, self.x_recv, self.y_sent, self.y_recv = scratch

    @staticmethod
    def scratch(*half):
        return [pltpu.VMEM((3,) + half, jnp.bfloat16)] * 2 + [pltpu.SemaphoreType.DMA((3,))] * 4

    def to_x(self, kind):
        dp, cp, z, core = self.where
        source = (
            self.part(dp ^ 3, 0) if kind == 0 else self.part(dp ^ 1, 0) if kind == 1 else self.work(1)
        )
        return send(
            source, self.from_x.at[kind], self.x_sent.at[kind], self.x_recv.at[kind], (dp ^ 1, cp)
        )

    def to_y(self, kind):
        dp, cp, z, core = self.where
        source = (
            self.part(dp ^ 3, 1) if kind == 0 else self.part(dp ^ 2, 1) if kind == 1 else self.work(0)
        )
        return send(
            source, self.from_y.at[kind], self.y_sent.at[kind], self.y_recv.at[kind], (dp ^ 2, cp)
        )

    def start(self):
        for kind in range(2):
            self.to_x(kind).start()
            self.to_y(kind).start()

    def add(self, index, *arrived):
        target = self.work(index)
        total = target[...].astype(jnp.float32)
        for block in arrived:
            total = total + block[...].astype(jnp.float32)
        target[...] = total.astype(jnp.bfloat16)

    def middle(self):
        self.to_x(0).wait_recv()
        self.add(0, self.from_x.at[0])
        self.to_y(2).start()
        self.to_y(0).wait_recv()
        self.add(1, self.from_y.at[0])
        self.to_x(2).start()

    def finish(self):
        for kind in (1, 2):
            self.to_x(kind).wait_recv()
            self.to_y(kind).wait_recv()
        self.add(2, self.from_x.at[1], self.from_y.at[2])
        self.add(3, self.from_y.at[1], self.from_x.at[2])

    def finish_send(self):
        for kind in range(3):
            self.to_x(kind).wait_send()
            self.to_y(kind).wait_send()

    def places(self):
        dp = self.where[0]
        return [(dp ^ 2, 0), (dp ^ 1, 1), (dp, 0), (dp, 1)]


def far_first(turn, z, depth):
    order = []
    for spot in range(depth):
        rest = sorted((other for other in range(depth) if other != spot), key=lambda other: (-abs(other - spot), other))
        ends = [other for other in rest if other in (0, depth - 1)]
        order.append(ends + [other for other in rest if other not in ends] + [spot])
    picked = 0
    for step in range(depth):
        for spot in range(depth):
            picked = picked + order[spot][step] * ((turn == step) & (z == spot)).astype(jnp.int32)
    return picked


def near_first(turn, z, depth):
    picked = 0
    for step in range(depth):
        for spot in range(depth):
            order = sorted(range(depth), key=lambda other: (abs(other - spot), other))
            picked = picked + order[step] * ((turn == step) & (z == spot)).astype(jnp.int32)
    return picked


def middle_kernel(
    own_ref,
    cotangent_in,
    gateup_in,
    down_in,
    d_normed_out,
    forward_out,
    down_out,
    gateup_out,
    normed,
    cotangent,
    gate_weight,
    up_weight,
    down_weight,
    hidden_up,
    d_gates,
    d_ups,
    parts,
    forwards,
    down_grad,
    gateup_grad,
    load_sems,
    save_sems,
    *scratch,
):
    where = place()
    dp, cp, z, core = where
    count, rows, width = normed.shape
    depth = count // 2
    tile = 2 * rows
    group_rows = count * rows
    loads = [
        pltpu.make_async_copy(source, target, load_sems.at[index])
        for index, (source, target) in enumerate(
            [
                (gateup_in.at[0], gate_weight),
                (gateup_in.at[1], up_weight),
                (cotangent_in, cotangent),
                (down_in, down_weight),
            ]
        )
    ]
    greet(
        [(dp, cp ^ turn) for turn in range(1, count)]
        + [(dp ^ 1, cp), (dp ^ 2, cp)]
    )
    second_line = LineGather(own_ref, normed, scratch[:5], where, depth)
    line = LineScatter(parts, d_normed_out, scratch[5:13], where, depth)
    lane_half = width // 2

    def down_part(d, h):
        return down_grad.at[d, :, pl.ds(h * lane_half, lane_half)]

    def down_work(index):
        return down_part(*down_ring.places()[index])

    down_ring = RingReduce(down_part, down_work, scratch[13:], where)
    second_line.start()
    for load in loads:
        load.start()
    at_end = (z == 0) | (z == depth - 1)
    for load in loads:
        load.wait()

    def feed(turn, carry):
        spot = near_first(turn, z, depth)
        far = jnp.abs(spot - z)

        @pl.when((turn > 0) & (far != jnp.abs(near_first(turn - 1, z, depth) - z)))
        def _():
            second_line.step(far)

        @pl.when(turn == 0)
        def _():
            second_line.keep().wait()

        second_line.arrive(spot)
        pair = pl.ds(2 * spot, 2)
        lanes = pl.ds(pl.multiple_of(spot * tile, tile), tile)
        block = normed[pair].reshape(tile, width)
        gate = jnp.dot(block, gate_weight[...], preferred_element_type=jnp.float32)
        up = jnp.dot(block, up_weight[...], preferred_element_type=jnp.float32)
        sig = 1.0 / (1.0 + jnp.exp(-gate))
        act = gate * sig
        hidden_up[:, lanes] = (act * up).T.astype(jnp.bfloat16)
        d_hidden = contract_cols(cotangent[pair].reshape(tile, width), down_weight[...])
        d_gate = (d_hidden * up * (sig * (1.0 + gate * (1.0 - sig)))).astype(jnp.bfloat16)
        d_up = (d_hidden * act).astype(jnp.bfloat16)
        d_gates[lanes] = d_gate
        d_ups[lanes] = d_up
        part = contract_cols(d_gate, gate_weight[...]) + contract_cols(d_up, up_weight[...])
        parts[pair] = part.astype(jnp.bfloat16).reshape(2, rows, width)
        line.pair(spot).start()

        @pl.when(at_end & (turn > 0))
        def _():
            line.forward(spot)

        return carry

    lax.fori_loop(0, depth, feed, 0)
    chunk = 256
    inner = depth - 1 - z
    outer = [inner, (depth - 1) * (z // 2 == 0).astype(jnp.int32), (depth - 1) * (z // 2 == 1).astype(jnp.int32)]

    def relay(index):
        @pl.when(jnp.logical_not(at_end))
        def _():
            line.forward(outer[index])

    def down_step(step, carry):
        lanes = pl.ds(pl.multiple_of(step * chunk, chunk), chunk)
        right = cotangent[:, :, lanes].reshape(group_rows, chunk)
        down_grad[:, :, lanes] = (
            jnp.dot(hidden_up[...], right, preferred_element_type=jnp.float32)
            .reshape(down_grad.shape[:2] + (chunk,))
            .astype(jnp.bfloat16)
        )
        return carry

    lax.fori_loop(0, width // chunk, down_step, 0)
    down_ring.start()
    relay(0)

    def gateup_step(step, carry):
        lanes = pl.ds(pl.multiple_of(step * chunk, chunk), chunk)
        left = normed[:, :, lanes].reshape(group_rows, chunk)
        gateup_grad[0, lanes] = contract_rows(left, d_gates[...]).astype(jnp.bfloat16)
        gateup_grad[1, lanes] = contract_rows(left, d_ups[...]).astype(jnp.bfloat16)
        return carry

    steps = width // chunk
    lax.fori_loop(0, steps // 2, gateup_step, 0)
    relay(1)
    lax.fori_loop(steps // 2, steps, gateup_step, 0)
    relay(2)
    saves = [pltpu.make_async_copy(gateup_grad, gateup_out, save_sems.at[0])]
    saves[0].start()
    down_ring.middle()

    def forward_step(step, carry):
        lanes = pl.ds(pl.multiple_of(step * tile, tile), tile)
        forwards[pl.ds(2 * step, 2)] = (
            contract_rows(hidden_up[:, lanes], down_weight[...])
            .astype(jnp.bfloat16)
            .reshape(2, rows, width)
        )
        return carry

    lax.fori_loop(0, depth, forward_step, 0)
    saves.append(pltpu.make_async_copy(forwards, forward_out, save_sems.at[1]))
    saves[1].start()
    line.finish()
    second_line.finish(True)
    down_ring.finish()
    for half in range(2):
        down_out[:, pl.ds(half * lane_half, lane_half)] = down_grad[
            dp, :, pl.ds(half * lane_half, lane_half)
        ].astype(jnp.float32)
    down_ring.finish_send()
    for save in saves:
        save.wait()


def middle(own, cotangent, gateup, down, data_count, collective_id):
    count, rows, width = cotangent.shape
    depth = count // 2
    hidden = down.shape[0]
    group_rows = count * rows
    bf = jnp.bfloat16
    any_space = pl.BlockSpec(memory_space=pl.ANY)
    in_vmem = pl.BlockSpec(memory_space=pltpu.VMEM)
    return pl.pallas_call(
        middle_kernel,
        out_shape=[
            jax.ShapeDtypeStruct((rows, width), jnp.float32),
            jax.ShapeDtypeStruct((count, rows, width), bf),
            jax.ShapeDtypeStruct((hidden // data_count, width), jnp.float32),
            jax.ShapeDtypeStruct((2, width, hidden), bf),
        ],
        in_specs=[in_vmem] + [any_space] * 3,
        out_specs=[in_vmem, any_space, in_vmem, any_space],
        scratch_shapes=[
            pltpu.VMEM((count, rows, width), bf),
            pltpu.VMEM((count, rows, width), bf),
            pltpu.VMEM((width, hidden), bf),
            pltpu.VMEM((width, hidden), bf),
            pltpu.VMEM((hidden, width), bf),
            pltpu.VMEM((hidden, group_rows), bf),
            pltpu.VMEM((group_rows, hidden), bf),
            pltpu.VMEM((group_rows, hidden), bf),
            pltpu.VMEM((count, rows, width), bf),
            pltpu.VMEM((count, rows, width), bf),
            pltpu.VMEM((data_count, hidden // data_count, width), bf),
            pltpu.VMEM((2, width, hidden), bf),
            pltpu.SemaphoreType.DMA((4,)),
            pltpu.SemaphoreType.DMA((2,)),
        ]
        + LineGather.scratch(depth)
        + LineScatter.scratch(depth, rows, width)
        + RingReduce.scratch(hidden // data_count, width // 2),
        compiler_params=pltpu.CompilerParams(
            collective_id=collective_id, has_side_effects=True, vmem_limit_bytes=60 * 2**20
        ),
        name="middle",
    )(own, cotangent, gateup, down)


def back_kernel(
    tokens_ref,
    cotangent_ref,
    residual_ref,
    d_normed_ref,
    gains_ref,
    order_ref,
    lengths_ref,
    cosine_ref,
    sine_ref,
    total_ref,
    normed_in,
    input_in,
    output_in,
    raw_in,
    flat_in,
    forward_in,
    gateup_in,
    mixed_out,
    token_out,
    gains_out,
    output_grad_out,
    input_grad_out,
    gateup_grad_out,
    inputs,
    outputs,
    raw,
    flat,
    forwards,
    forward_sum,
    d_first,
    d_residual,
    branch,
    swap_send,
    swap_recv,
    queries,
    keys,
    keys_up,
    values_up,
    d_query,
    d_key,
    d_value,
    d_projected,
    parts,
    input_grad,
    output_sib,
    output_line,
    gateup_work,
    gain_sums,
    own_gains,
    line_gains,
    all_gains,
    key_place_ref,
    query_place_ref,
    query_start_ref,
    load_sems,
    work_sems,
    share_sems,
    output_sent,
    output_recv,
    line_sent,
    line_recv,
    all_sent,
    all_recv,
    *scratch,
):
    where = place()
    dp, cp, z, core = where
    count, rows, width = forwards.shape
    depth = count // 2
    data_count = all_gains.shape[0]
    shard = inputs.shape[2]
    tile = 2 * rows
    group_rows = count * rows
    heads = HEADS // KV_HEADS
    q_each = heads * HEAD_DIM
    flat_width = HEADS * HEAD_DIM
    score_scale = HEAD_DIM ** (-0.5)
    load_pairs = [
        (output_in, outputs),
        (raw_in, raw),
        (forward_in, forwards),
        (flat_in, flat),
        (normed_in, forwards),
        (input_in, inputs),
    ]
    loads = [
        pltpu.make_async_copy(source, target, load_sems.at[index])
        for index, (source, target) in enumerate(load_pairs)
    ]
    for index in (0, 1, 2, 3, 5):
        loads[index].start()
    greet(
        [(dp, cp ^ turn) for turn in range(1, count)]
        + [(dp ^ turn, cp) for turn in range(1, data_count)]
    )
    swap = Swap(swap_send, swap_recv, scratch[:3], where, count)
    take = iter(scratch[3:])

    def some(amount):
        return [next(take) for _ in range(amount)]

    forward_line = LineScatter(forwards, forward_sum, some(8), where, depth)
    first_line = LineScatter(parts, d_first, some(8), where, depth)
    gateup_rows = data_count * count * shard // data_count

    def in_place(part):
        spots = [(dp ^ 2, 0), (dp ^ 1, 1), (dp, 0), (dp, 1)]
        return lambda index: part(*spots[index])

    gateup_half = gateup_rows // 2

    def gateup_part(index):
        return lambda d, h: gateup_in.at[
            index, pl.ds(pl.multiple_of(d * gateup_rows + h * gateup_half, 16), gateup_half)
        ]

    def gateup_ring(index):
        return RingReduce(
            gateup_part(index), lambda spot: gateup_work.at[index, spot], some(6), where
        )

    def gateup_own(index):
        each = gateup_half // shard
        return lambda slot: gateup_work.at[
            index, 2 + slot // each, pl.ds(pl.multiple_of(slot % each * shard, 16), shard)
        ]

    def output_part(d, h):
        return outputs.at[d, pl.ds(h * (depth // 2), depth // 2), core]

    def input_part(d, h):
        half = gateup_rows // 2
        return input_grad.at[pl.ds(pl.multiple_of(d * gateup_rows + h * half, 16), half)]

    gate_ring, up_ring = gateup_ring(0), gateup_ring(1)
    output_ring = RingReduce(output_part, in_place(output_part), some(6), where)
    input_ring = RingReduce(input_part, in_place(input_part), some(6), where)

    def own_shard(source):
        return lambda slot: source.at[pl.ds(pl.multiple_of(slot * shard, 16), shard)]

    gate_swap = Swap(gateup_own(0), gateup_grad_out.at[0], some(3), where, count)
    up_swap = Swap(gateup_own(1), gateup_grad_out.at[1], some(3), where, count)
    own_rows = input_grad.at[pl.ds(pl.multiple_of(dp * gateup_rows, 16), gateup_rows)]
    input_swap = Swap(own_shard(own_rows), input_grad_out, some(3), where, count)
    works = [
        pltpu.make_async_copy(ring.part(*spot), ring.work(index), work_sems.at[4 * turn + index])
        for turn, ring in enumerate((gate_ring, up_ring))
        for index, spot in enumerate(ring.places())
    ]
    gate_ring.start()
    for work in works:
        work.start()

    def share(mine):
        return send(
            outputs.at[:, :, 1 - core], output_sib, share_sems.at[0], share_sems.at[1], (dp, cp ^ 1)
        )

    def output_hop(far, mine):
        return send(
            outputs.at[dp, z ^ far, core],
            output_line.at[z if mine else z ^ far],
            output_sent.at[far],
            output_recv.at[far],
            (dp, cp ^ (2 * far)),
        )

    at_end = (z == 0) | (z == depth - 1)
    chunk = 256

    gain_one, gain_two, gain_query, gain_key = split_gains(gains_ref, width)
    hat_two, inv_two = rms_parts(residual_ref[...])
    d_normed = d_normed_ref[...]
    own_gains[:, pl.ds(width, width)] = jnp.sum(d_normed * hat_two, axis=0, keepdims=True)
    d_res = cotangent_ref[...].astype(jnp.float32) + norm_back(
        d_normed * gain_two, hat_two, inv_two
    )
    d_residual[...] = d_res
    branch[...] = d_res.astype(jnp.bfloat16)
    loads[0].wait()
    swap_send[...] = (
        contract_cols(outputs[...].reshape(flat_width, width), branch[...])
        .astype(jnp.bfloat16)
        .reshape(count, q_each, rows)
    )
    swap.start()
    loads[2].wait()
    for spot in forward_line.order():
        forward_line.pair(spot).start()
    loads[1].wait()

    def prepare(turn, carry):
        lanes = pl.ds(pl.multiple_of(turn * tile, tile), tile)
        cosine, sine = cosine_ref[:, lanes], sine_ref[:, lanes]
        for head in range(heads):
            spot = pl.ds(head * HEAD_DIM, HEAD_DIM)
            hat, _ = head_hat(raw[spot, lanes])
            queries[spot, lanes] = turn_heads(hat * gain_query, cosine, sine).astype(
                jnp.bfloat16
            )
        hat, _ = head_hat(raw[pl.ds(q_each, HEAD_DIM), lanes])
        key = turn_heads(hat * gain_key, cosine, sine)
        keys[:, lanes] = key.astype(jnp.bfloat16)
        keys_up[lanes] = key.T.astype(jnp.bfloat16)
        values_up[lanes] = raw[pl.ds(q_each + HEAD_DIM, HEAD_DIM), lanes].T.astype(jnp.bfloat16)
        return carry

    lax.fori_loop(0, depth, prepare, 0)
    place_row, place_column, starts = lay_places(order_ref, lengths_ref, rows, count)
    query_place_ref[...] = place_row
    key_place_ref[...] = place_column
    query_start_ref[...] = starts
    d_key[...] = jnp.zeros_like(d_key)
    d_value[...] = jnp.zeros_like(d_value)
    gain_sums[...] = jnp.zeros_like(gain_sums)

    @pl.when(at_end)
    def _():
        for turn in range(depth - 1):
            forward_line.forward(far_first(turn, z, depth))

    loads[3].wait()

    def output_step(step, carry):
        lanes = pl.ds(pl.multiple_of(step * chunk, chunk), chunk)
        outputs[:, :, :, :, lanes] = (
            jnp.dot(
                flat[...].reshape(flat_width, rows),
                branch[:, lanes],
                preferred_element_type=jnp.float32,
            )
            .astype(jnp.bfloat16)
            .reshape(outputs.shape[:4] + (chunk,))
        )
        return carry

    lax.fori_loop(0, width // chunk, output_step, 0)
    share(True).start()
    for work in works:
        work.wait()
    gate_ring.middle()
    up_ring.start()
    swap.finish_recv()

    def attend(turn, carry):
        lanes = pl.ds(pl.multiple_of(turn * tile, tile), tile)
        query_place, query_start = query_place_ref[:, lanes], query_start_ref[:, lanes]

        @pl.when(jnp.logical_not(at_end) & (turn >= 1))
        def _():
            forward_line.forward(far_first(turn - 1, z, depth))

        @pl.when(turn == 1)
        def _():
            gate_ring.finish()
            gate_swap.start()

        @pl.when(turn == 3)
        def _():
            up_ring.middle()

        for head in range(heads):
            spot = pl.ds(head * HEAD_DIM, HEAD_DIM)
            scores, allowed = score_block(
                keys_up[...], queries[spot, lanes], key_place_ref[...], query_place, query_start
            )
            probs = jnp.where(allowed, jnp.exp(scores - total_ref[pl.ds(head, 1), lanes]), 0.0)
            d_out = jnp.concatenate(
                [swap_recv[2 * turn, spot], swap_recv[2 * turn + 1, spot]], axis=1
            )
            d_probs = jnp.dot(values_up[...], d_out, preferred_element_type=jnp.float32)
            delta = jnp.sum(probs * d_probs, axis=0, keepdims=True)
            d_scores = (probs * (d_probs - delta)).astype(jnp.bfloat16)
            d_query[spot, lanes] = (
                jnp.dot(keys[...], d_scores, preferred_element_type=jnp.float32) * score_scale
            )
            d_key[...] += contract_cols(queries[spot, lanes], d_scores) * score_scale
            d_value[...] += contract_cols(d_out, probs.astype(jnp.bfloat16))
        return carry

    lax.fori_loop(0, depth, attend, 0)
    loads[5].wait()
    share(False).wait_recv()

    def share_step(step, carry):
        total = outputs[step, :, core].astype(jnp.float32) + output_sib[step].astype(jnp.float32)
        outputs[step, :, core] = total.astype(jnp.bfloat16)
        return carry

    lax.fori_loop(0, data_count, share_step, 0)
    output_ring.start()

    def feed(turn, carry):
        spot = far_first(turn, z, depth)
        lanes = pl.ds(pl.multiple_of(spot * tile, tile), tile)
        cosine, sine = cosine_ref[:, lanes], sine_ref[:, lanes]
        pieces = []
        for head in range(heads + 1):
            place_in = pl.ds(head * HEAD_DIM, HEAD_DIM)
            hat, inverse = head_hat(raw[place_in, lanes])
            if head < heads:
                turned = turn_heads(d_query[place_in, lanes], cosine, -sine)
                gain, kind = gain_query, 0
            else:
                turned = turn_heads(d_key[:, lanes], cosine, -sine)
                gain, kind = gain_key, 1
            gain_sums[kind] += turned * hat
            scaled = turned * gain
            pieces.append(
                inverse * (scaled - hat * jnp.mean(scaled * hat, axis=0, keepdims=True))
            )
        pieces.append(d_value[:, lanes])
        block = jnp.concatenate(pieces, axis=0).T.astype(jnp.bfloat16)
        d_projected[lanes] = block
        part = contract_cols(block, inputs[...].reshape(width, block.shape[1]))
        parts[pl.ds(2 * spot, 2)] = part.astype(jnp.bfloat16).reshape(2, rows, width)
        first_line.pair(spot).start()

        @pl.when(at_end & (turn < depth - 1))
        def _():
            first_line.forward(spot)

        return carry

    lax.fori_loop(0, depth, feed, 0)
    up_ring.finish()
    up_swap.start()
    forward_line.finish()
    loads[4].start()
    mixed_out[...] = (residual_ref[...] + forward_sum[...]).astype(jnp.bfloat16)
    for kind in range(2):
        own_gains[:, pl.ds(2 * width + kind * HEAD_DIM, HEAD_DIM)] = jnp.sum(
            gain_sums[kind].T, axis=0, keepdims=True
        )
    @pl.when(jnp.logical_not(at_end))
    def _():
        first_line.forward(far_first(0, z, depth))

    loads[4].wait()

    def input_step(step, carry):
        lanes = pl.ds(pl.multiple_of(step * chunk, chunk), chunk)
        left = forwards[:, :, lanes].reshape(group_rows, chunk)
        input_grad[lanes] = contract_rows(left, d_projected[...]).astype(jnp.bfloat16)
        return carry

    lax.fori_loop(0, width // chunk, input_step, 0)
    input_ring.start()
    output_ring.middle()

    @pl.when(jnp.logical_not(at_end))
    def _():
        first_line.forward(far_first(1, z, depth))

    input_ring.middle()

    @pl.when(jnp.logical_not(at_end))
    def _():
        first_line.forward(far_first(2, z, depth))

    output_ring.finish()
    for far in range(depth - 1, 0, -1):
        output_hop(far, True).start()
    input_ring.finish()
    input_swap.start()
    first_line.finish()
    hat_one, inv_one = rms_parts(tokens_ref[...].astype(jnp.float32))
    d_one = d_first[...]
    own_gains[:, pl.ds(0, width)] = jnp.sum(d_one * hat_one, axis=0, keepdims=True)
    line_gains[cp] = own_gains[...]
    for turn in range(1, count):
        send(
            own_gains, line_gains.at[cp], line_sent.at[turn], line_recv.at[turn], (dp, cp ^ turn)
        ).start()
    token_out[...] = d_residual[...] + norm_back(d_one * gain_one, hat_one, inv_one)
    for turn in range(1, count):
        copy = send(
            own_gains,
            line_gains.at[cp ^ turn],
            line_sent.at[turn],
            line_recv.at[turn],
            (dp, cp ^ turn),
        )
        copy.wait_recv()
        copy.wait_send()
    all_gains[dp] = jnp.sum(line_gains[...], axis=0)
    for turn in range(1, data_count):
        send(
            all_gains.at[dp],
            all_gains.at[dp],
            all_sent.at[turn],
            all_recv.at[turn],
            (dp ^ turn, cp),
        ).start()
    for turn in range(1, data_count):
        copy = send(
            all_gains.at[dp],
            all_gains.at[dp ^ turn],
            all_sent.at[turn],
            all_recv.at[turn],
            (dp ^ turn, cp),
        )
        copy.wait_recv()
        copy.wait_send()
    gains_out[...] = jnp.sum(all_gains[...], axis=0)
    total = outputs[dp, z, core].astype(jnp.float32)
    for far in range(1, depth):
        output_hop(far, False).wait_recv()
        total = total + output_line[z ^ far].astype(jnp.float32)
    output_grad_out[...] = total
    for done in (input_swap, gate_swap, up_swap):
        done.finish_recv()
    for done in (swap, input_swap, gate_swap, up_swap, gate_ring, up_ring, output_ring, input_ring):
        done.finish_send()
    for far in range(1, depth):
        output_hop(far, True).wait_send()
    share(True).wait_send()


def back(
    tokens,
    cotangent,
    residual,
    d_normed,
    gains,
    order,
    lengths,
    cosine,
    sine,
    log_total,
    normed,
    inputs,
    outputs,
    raw,
    flat,
    forwards,
    gateup_grad,
    collective_id,
):
    count, rows, width = normed.shape
    depth = count // 2
    data_count = inputs.shape[0]
    shard, each = inputs.shape[2:]
    hidden = gateup_grad.shape[2]
    group_rows = count * rows
    heads = HEADS // KV_HEADS
    q_each = heads * HEAD_DIM
    flat_width = HEADS * HEAD_DIM
    gain_width = 2 * width + 2 * HEAD_DIM
    bf = jnp.bfloat16
    f32 = jnp.float32
    any_space = pl.BlockSpec(memory_space=pl.ANY)
    in_vmem = pl.BlockSpec(memory_space=pltpu.VMEM)
    in_smem = pl.BlockSpec(memory_space=pltpu.SMEM)
    return pl.pallas_call(
        back_kernel,
        out_shape=[
            jax.ShapeDtypeStruct((rows, width), bf),
            jax.ShapeDtypeStruct((rows, width), f32),
            jax.ShapeDtypeStruct((1, gain_width), f32),
            jax.ShapeDtypeStruct((shard, width), f32),
            jax.ShapeDtypeStruct((count, shard, each), bf),
            jax.ShapeDtypeStruct((2, count, shard, hidden), bf),
        ],
        in_specs=[in_vmem] * 5 + [in_smem] * 2 + [in_vmem] * 3 + [any_space] * 7,
        out_specs=[in_vmem] * 4 + [any_space] * 2,
        scratch_shapes=[
            pltpu.VMEM(inputs.shape, bf),
            pltpu.VMEM(outputs.shape, bf),
            pltpu.VMEM(raw.shape, f32),
            pltpu.VMEM(flat.shape, bf),
            pltpu.VMEM(forwards.shape, bf),
            pltpu.VMEM((rows, width), f32),
            pltpu.VMEM((rows, width), f32),
            pltpu.VMEM((rows, width), f32),
            pltpu.VMEM((rows, width), bf),
            pltpu.VMEM((count, q_each, rows), bf),
            pltpu.VMEM((count, q_each, rows), bf),
            pltpu.VMEM((q_each, group_rows), bf),
            pltpu.VMEM((HEAD_DIM, group_rows), bf),
            pltpu.VMEM((group_rows, HEAD_DIM), bf),
            pltpu.VMEM((group_rows, HEAD_DIM), bf),
            pltpu.VMEM((q_each, group_rows), f32),
            pltpu.VMEM((HEAD_DIM, group_rows), f32),
            pltpu.VMEM((HEAD_DIM, group_rows), f32),
            pltpu.VMEM((group_rows, each), bf),
            pltpu.VMEM(forwards.shape, bf),
            pltpu.VMEM((width, each), bf),
            pltpu.VMEM((data_count, depth, shard, width), bf),
            pltpu.VMEM((depth, shard, width), bf),
            pltpu.VMEM((2, 4, count * shard // 2, hidden), bf),
            pltpu.VMEM((2, HEAD_DIM, 2 * rows), f32),
            pltpu.VMEM((1, gain_width), f32),
            pltpu.VMEM((count, 1, gain_width), f32),
            pltpu.VMEM((data_count, 1, gain_width), f32),
            pltpu.VMEM((group_rows, 1), jnp.int32),
            pltpu.VMEM((1, group_rows), jnp.int32),
            pltpu.VMEM((1, group_rows), jnp.int32),
            pltpu.SemaphoreType.DMA((6,)),
            pltpu.SemaphoreType.DMA((8,)),
            pltpu.SemaphoreType.DMA((2,)),
            pltpu.SemaphoreType.DMA((depth,)),
            pltpu.SemaphoreType.DMA((depth,)),
            pltpu.SemaphoreType.DMA((count,)),
            pltpu.SemaphoreType.DMA((count,)),
            pltpu.SemaphoreType.DMA((data_count,)),
            pltpu.SemaphoreType.DMA((data_count,)),
        ]
        + Swap.scratch(count)
        + LineScatter.scratch(depth, rows, width) * 2
        + RingReduce.scratch(count * shard // 2, hidden) * 2
        + RingReduce.scratch(depth // 2, shard, width)
        + RingReduce.scratch(count * shard // 2, each)
        + Swap.scratch(count) * 3,
        compiler_params=pltpu.CompilerParams(
            collective_id=collective_id, has_side_effects=True, vmem_limit_bytes=63 * 2**20
        ),
        name="back",
    )(
        tokens,
        cotangent,
        residual,
        d_normed,
        gains,
        order,
        lengths,
        cosine,
        sine,
        log_total,
        normed,
        inputs,
        outputs,
        raw,
        flat,
        forwards,
        gateup_grad,
    )


def update_kernel(
    data_count,
    gateup_grad,
    input_grad,
    output_grad,
    down_grad,
    gains_grad,
    *refs,
):
    states, results = refs[:15], refs[15:30]
    scratch = refs[30]
    input_full = refs[31]
    context_count = gateup_grad.shape[1]
    piece = gateup_grad.shape[3] // data_count
    half = scratch.shape[1] // 2
    for side in range(2):
        for group in range(data_count):
            scratch[:, pl.ds(side * half + group * context_count * piece, context_count * piece)] = (
                jnp.concatenate(
                    [
                        gateup_grad[side, head, :, pl.ds(group * piece, piece)]
                        for head in range(context_count)
                    ],
                    axis=1,
                ).astype(jnp.float32)
            )
    q_each = HEADS // KV_HEADS * HEAD_DIM
    for start, size in ((0, q_each), (q_each, HEAD_DIM), (q_each + HEAD_DIM, HEAD_DIM)):
        input_full[:, pl.ds(start * context_count, size * context_count)] = jnp.concatenate(
            [input_grad[head, :, pl.ds(start, size)] for head in range(context_count)], axis=1
        ).astype(jnp.float32)
    jobs = (
        (input_full, rate_input, weight_decay),
        (output_grad, rate_output, weight_decay),
        (scratch, rate_gateup, weight_decay),
        (down_grad, rate_down, weight_decay),
        (gains_grad, rate_gains, 0.0),
    )
    for index, (gradient, rate, decay) in enumerate(jobs):
        weight, first, second = (state[...] for state in states[3 * index : 3 * index + 3])
        for result, value in zip(
            results[3 * index : 3 * index + 3],
            adam_update(weight, first, second, gradient[...], rate, decay),
        ):
            result[...] = value


def update(gateup_grad, input_grad, output_grad, down_grad, gains_grad, states, data_count):
    parts = 3

    def rows_of(array):
        axis = array.ndim - 2
        shape = list(array.shape)
        if shape[axis] > 1:
            shape[axis] //= parts
            return pl.BlockSpec(
                tuple(shape), lambda step: tuple(step if d == axis else 0 for d in range(len(shape)))
            )
        return pl.BlockSpec(tuple(shape), lambda step: (0,) * len(shape))

    arrays = [gateup_grad, input_grad, output_grad, down_grad, gains_grad] + list(states)
    shard = states[0].shape[0] // parts
    return pl.pallas_call(
        functools.partial(update_kernel, data_count),
        grid=(parts,),
        out_shape=[jax.ShapeDtypeStruct(state.shape, jnp.float32) for state in states],
        in_specs=[rows_of(array) for array in arrays],
        out_specs=[rows_of(state) for state in states],
        scratch_shapes=[
            pltpu.VMEM((shard, states[6].shape[1]), jnp.float32),
            pltpu.VMEM((shard, states[0].shape[1]), jnp.float32),
        ],
        compiler_params=pltpu.CompilerParams(vmem_limit_bytes=56 * 2**20),
        name="update",
    )(*arrays)


def on_device_split(
    tokens,
    output_cotangent,
    sequence_lengths,
    block_order,
    attn_input,
    input_moment,
    input_square,
    attn_output,
    output_moment,
    output_square,
    gate_up,
    gateup_moment,
    gateup_square,
    down_weight,
    down_moment,
    down_square,
    norm_gains,
    gains_moment,
    gains_square,
):
    context_count = lax.axis_size("cp")
    data_count = lax.axis_size("dp")
    model_width = tokens.shape[1]
    gains_row = norm_gains.reshape(1, -1)
    down_part = lax.all_gather(down_weight.astype(jnp.bfloat16), "dp", axis=0, tiled=True)
    (
        normed_one,
        own_two,
        cotangent_all,
        input_part,
        output_all,
        gateup_part,
        raw,
        flat_parts,
        log_total,
        residual,
        cosine,
        sine,
    ) = front(
        tokens,
        gains_row,
        block_order,
        sequence_lengths,
        attn_input,
        attn_output,
        gate_up,
        output_cotangent,
        data_count,
        context_count,
    )
    d_normed_two, forward_parts, grad_down, gateup_grad = middle(
        own_two,
        cotangent_all,
        gateup_part.reshape(2, model_width, -1),
        down_part,
        data_count,
        3,
    )
    mixed, token_gradient, grad_gains, grad_output, grad_input, grad_gateup = back(
        tokens,
        output_cotangent,
        residual,
        d_normed_two,
        gains_row,
        block_order,
        sequence_lengths,
        cosine,
        sine,
        log_total,
        normed_one,
        input_part,
        output_all,
        raw,
        flat_parts,
        forward_parts,
        gateup_grad,
        4,
    )
    states = (
        attn_input,
        input_moment,
        input_square,
        attn_output,
        output_moment,
        output_square,
        gate_up,
        gateup_moment,
        gateup_square,
        down_weight,
        down_moment,
        down_square,
        gains_row,
        gains_moment.reshape(1, -1),
        gains_square.reshape(1, -1),
    )
    results = update(
        grad_gateup, grad_input, grad_output, grad_down, grad_gains, states, data_count
    )
    return (
        mixed,
        token_gradient,
        *results[:12],
        *(result.reshape(-1) for result in results[12:]),
    )


def solution(mesh):
    in_specs = (
        P(("dp", "cp"), None),
        P(("dp", "cp"), None),
        P("dp", None),
        P("dp", None),
        P(("dp", "cp"), None),
        P(("dp", "cp"), None),
        P(("dp", "cp"), None),
        P(("dp", "cp"), None),
        P(("dp", "cp"), None),
        P(("dp", "cp"), None),
        P(("dp", "cp"), None),
        P(("dp", "cp"), None),
        P(("dp", "cp"), None),
        P(("dp", "cp"), None),
        P(("dp", "cp"), None),
        P(("dp", "cp"), None),
        P(),
        P(),
        P(),
    )
    out_specs = (
        P(("dp", "cp"), None),
        P(("dp", "cp"), None),
        P(("dp", "cp"), None),
        P(("dp", "cp"), None),
        P(("dp", "cp"), None),
        P(("dp", "cp"), None),
        P(("dp", "cp"), None),
        P(("dp", "cp"), None),
        P(("dp", "cp"), None),
        P(("dp", "cp"), None),
        P(("dp", "cp"), None),
        P(("dp", "cp"), None),
        P(("dp", "cp"), None),
        P(("dp", "cp"), None),
        P(),
        P(),
        P(),
    )
    sizes = (mesh.shape["dp"], mesh.shape["cp"])
    body = on_device_split if sizes == (4, KV_HEADS) else on_device
    return jax.shard_map(
        body, mesh=mesh, in_specs=in_specs, out_specs=out_specs, check_vma=False
    )
```

profile of v0, /device:TPU:0, one launch (start us, length us, event | category | flops | bytes accessed | tf_op | source)
XLA Modules:
  0.0 345.5 jit_solution(8304125921792569743)
XLA Ops:
  7.2 0.0 copy-start.2
  7.2 0.0 copy-start.3
  7.2 0.0 copy-start.4
  7.2 0.0 all-gather.2.cloned.1.call-start
  7.3 2.2 convert_element_type.3
  9.5 0.0 all-gather.2.cloned.1.call-update
  9.5 0.0 copy-done.2
  9.5 0.6 reshape.55.gains_ref.refs_12_
  10.1 0.0 copy-done.3
  10.1 0.6 reshape.57.refs_13_
  10.8 0.0 copy-done.4
  10.8 0.6 reshape.58.refs_14_
  11.4 123.7 %front.1 = (bf16[8,128,1536]{2,1,0:T(8,128)(2,1)}, bf16[128,1536]{1,0:T(8,128)(2,1)}, bf16[8,128,1536]{2,1,0:T(8,128)(2,1)}, bf16[4,8,48,320]{3,2,1,0:T(8,128)(2...) custom-call(bf16[128,1536]{1,0:T(8,128)(2,1)} %tokens_ref.3, ...), custom_call_target="tpu_custom_call" | custom-call | tf_op jit(solution)/shard_map/front/pallas_call | solution.py:953
  135.1 0.0 all-gather.2.cloned.1.call-done.down_in
  135.1 71.7 %middle.1 = (f32[128,1536]{1,0:T(8,128)}, bf16[8,128,1536]{2,1,0:T(8,128)(2,1)}, f32[216,1536]{1,0:T(8,128)}, bf16[2,1536,864]{2,1,0:T(8,128)(2,1)}) custom-call(bf16[128,1536]{1,0:T(8,128)(2,1)} %get-tuple-element.55.own_ref, bf16[8,128,1536]{2,1,0:T(8,128)(2,1)} %get-tuple-element.56.cotangent_in, bf16[2,1536,864]{2,1,0:T(8,128)(2,1)} %bitcast.1, ...), custom_call_target="tpu_custom_call" | custom-call | tf_op jit(solution)/shard_map/middle/pallas_call | solution.py:1385
  206.8 113.0 %back.1 = (bf16[128,1536]{1,0:T(8,128)(2,1)}, f32[128,1536]{1,0:T(8,128)}, f32[1,3200]{1,0:T(1,128)}, f32[48,1536]{1,0:T(8,128)}, bf16[8,48,320]{2,1,0:T(8,128)(2,1)}, /*index=5*/bf16[2,8,48,864]{3,2,1,0:T(8,128)(2,1)}) custom-call(bf16[128,1536]{1,0:T(8,128)(2,1)} %tokens_ref.3, bf16[128,1536]{1,0:T(8,128)(2,1)} %cotangent_ref.1, ...), custom_call_target="tpu_custom_call" | custom-call | tf_op jit(solution)/shard_map/back/pallas_call | solution.py:1877
  319.9 0.0 copy-start.1
  319.9 0.0 copy-start
  319.9 13.1 %update.1 = (f32[48,2560]{1,0:T(8,128)}, f32[48,2560]{1,0:T(8,128)}, f32[48,2560]{1,0:T(8,128)}, f32[48,1536]{1,0:T(8,128)}, f32[48,1536]{1,0:T(8,128)}, /*index...) custom-call(bf16[2,8,48,864]{3,2,1,0:T(8,128)(2,1)} %get-tuple-eleme, ...), custom_call_target="tpu_custom_call" | custom-call | tf_op jit(solution)/shard_map/update/pallas_call | solution.py:2024
  333.0 1.4 reduce
  334.4 1.3 reduce.1
  335.7 1.3 reduce.2
  337.1 0.7 copy.38
  337.8 0.9 copy.39
  (2 shorter events, 0.0 us)
Async XLA Ops:
  7.2 2.3 copy-start.2
  7.2 2.9 copy-start.3
  7.2 3.5 %copy-start.4 = (f32[3200]{0:T(1024)S(1)}, f32[3200]{0:T(1024)}, u32[]{:S(2)}) copy-start(f32[3200]{0:T(1024)} %param.37) | copy-start | bytes 38404
  7.2 127.9 %all-gather.2.cloned.1.call-start = ((), (), s32[]{:S(2)}) async-start(), calls=%async_computation | async-start | bytes 3317760 | tf_op jit(solution)/shard_map/all_gather | solution.py:2064
  319.9 17.2 %copy-start.1 = (bf16[128,1536]{1,0:T(8,128)(2,1)S(1)}, bf16[128,1536]{1,0:T(8,128)(2,1)}, u32[]{:S(2)}) copy-start(bf16[128,1536]{1,0:T(8,128)(2,1)} %get-tuple-element.108) | copy-start | bytes 1179652
  319.9 17.9 %copy-start = (f32[128,1536]{1,0:T(8,128)S(1)}, f32[128,1536]{1,0:T(8,128)}, u32[]{:S(2)}) copy-start(f32[128,1536]{1,0:T(8,128)} %get-tuple-element.109) | copy-start | bytes 2359300
Sparse Core Ops, SparseCore 0:
  10.5 57.9 all-gather.1
where the time goes:
time: 346 us
  Pallas kernels  322 us (93%)
  between operations  14.1 us (4%)
  other arithmetic  6.28 us (2%)
  local copies, waits for them, and re-layouts  3.47 us (1%)
    pallas_call x1, Pallas kernels, front(): pl.pallas_call(functools.partial(front_kernel, 2 * rows), out_shape=[jax....  124 us
    pallas_call x1, Pallas kernels, back(): pl.pallas_call(back_kernel, out_shape=[jax.ShapeDtypeStruct((rows, width)...  113 us
    pallas_call x1, Pallas kernels, middle(): pl.pallas_call(middle_kernel, out_shape=[jax.ShapeDtypeStruct((rows, widt...  71.7 us
    pallas_call x1, Pallas kernels, update(): pl.pallas_call(functools.partial(update_kernel, data_count), grid=(parts,...  13.1 us
  transfers between devices with their start and end apart: 1, of which 0 were waited for; matrix products, arithmetic and copies ran while one was open for 1% of the time, Pallas kernels for 36%

commit v1 on v0

--- a/solution.py
+++ b/solution.py
@@ -643,10 +643,15 @@
 
 
 def split_gains(gains_ref, width):
-    gain_one = gains_ref[:, :width]
-    gain_two = gains_ref[:, width : 2 * width]
-    gain_query = to_column(gains_ref[:, 2 * width : 2 * width + HEAD_DIM])
-    gain_key = to_column(gains_ref[:, 2 * width + HEAD_DIM :])
+    lines = width // gains_ref.shape[1]
+
+    def row(begin, end):
+        return jnp.concatenate([gains_ref[line : line + 1] for line in range(begin, end)], axis=1)
+
+    gain_one, gain_two = row(0, lines), row(lines, 2 * lines)
+    gain_heads = row(2 * lines, gains_ref.shape[0])
+    gain_query = to_column(gain_heads[:, :HEAD_DIM])
+    gain_key = to_column(gain_heads[:, HEAD_DIM:])
     return gain_one, gain_two, gain_query, gain_key
 
 
@@ -656,7 +661,231 @@
     return jnp.where(allowed, scores, masked_score), allowed
 
 
-def front_kernel(
+class LineScatter:
+    cuts = 2
+
+    def __init__(self, part_ref, out_ref, scratch, where, depth):
+        self.part, self.out, self.where, self.depth = part_ref, out_ref, where, depth
+        self.sib, self.line = scratch[:2]
+        (
+            self.sib_sent,
+            self.sib_recv,
+            self.right_sent,
+            self.right_recv,
+            self.left_sent,
+            self.left_recv,
+        ) = scratch[2:]
+        self.size = part_ref.shape[1] // self.cuts
+
+    @classmethod
+    def scratch(cls, depth, rows, width):
+        return [
+            pltpu.VMEM((depth, rows, width), jnp.bfloat16),
+            pltpu.VMEM((depth + 1, rows, width), jnp.bfloat16),
+        ] + [pltpu.SemaphoreType.DMA((depth,))] * 2 + [
+            pltpu.SemaphoreType.DMA((depth * cls.cuts,))
+        ] * 4
+
+    def pair(self, spot):
+        dp, cp, z, core = self.where
+        return send(
+            self.part.at[2 * spot + 1 - core],
+            self.sib.at[spot],
+            self.sib_sent.at[spot],
+            self.sib_recv.at[spot],
+            (dp, cp ^ 1),
+        )
+
+    def rows(self, cut):
+        return pl.ds(cut * self.size, self.size)
+
+    def hop_right(self, spot, cut):
+        dp, cp, z, core = self.where
+        index = spot * self.cuts + cut
+        return send(
+            self.part.at[2 * spot + core, self.rows(cut)],
+            self.line.at[spot + 1, self.rows(cut)],
+            self.right_sent.at[index],
+            self.right_recv.at[index],
+            (dp, cp + 2),
+        )
+
+    def hop_left(self, spot, cut):
+        dp, cp, z, core = self.where
+        index = spot * self.cuts + cut
+        return send(
+            self.part.at[2 * spot + core, self.rows(cut)],
+            self.line.at[spot, self.rows(cut)],
+            self.left_sent.at[index],
+            self.left_recv.at[index],
+            (dp, cp - 2),
+        )
+
+    def order(self):
+        spots = []
+        for turn in range(self.depth):
+            spots += [self.depth - 1 - turn, turn]
+        return list(dict.fromkeys(spots))
+
+    def chip_sum(self, spot, cut):
+        rows = self.rows(cut)
+        mine = self.part[2 * spot + self.where[3], rows].astype(jnp.float32)
+        return mine + self.sib[spot, rows].astype(jnp.float32)
+
+    def pass_on(self, spot, cut, arrived, slot, hop):
+        total = self.chip_sum(spot, cut)
+        if arrived is not None:
+            arrived.wait_recv()
+            total = total + self.line[slot, self.rows(cut)].astype(jnp.float32)
+        self.part[2 * spot + self.where[3], self.rows(cut)] = total.astype(jnp.bfloat16)
+        hop.start()
+
+    def forward(self, spot, cuts=None):
+        z, core = self.where[2], self.where[3]
+        cuts = range(self.cuts) if cuts is None else cuts
+        if 0 in cuts:
+
+            @pl.when(z != spot)
+            def _():
+                self.pair(spot).wait_recv()
+
+        for cut in cuts:
+            right, left = self.hop_right(spot, cut), self.hop_left(spot, cut)
+
+            @pl.when((z < spot) & (z > 0))
+            def _():
+                self.pass_on(spot, cut, right, spot + 1, right)
+
+            @pl.when((z < spot) & (z == 0))
+            def _():
+                self.pass_on(spot, cut, None, None, right)
+
+            @pl.when((z > spot) & (z < self.depth - 1))
+            def _():
+                self.pass_on(spot, cut, left, spot, left)
+
+            @pl.when((z > spot) & (z == self.depth - 1))
+            def _():
+                self.pass_on(spot, cut, None, None, left)
+
+    def finish(self):
+        z = self.where[2]
+        self.pair(z).wait_recv()
+        for cut in range(self.cuts):
+            rows = self.rows(cut)
+            self.out[rows] = self.chip_sum(z, cut)
+
+            @pl.when(z > 0)
+            def _():
+                self.hop_right(z, cut).wait_recv()
+                self.out[rows] += self.line[z + 1, rows].astype(jnp.float32)
+
+            @pl.when(z < self.depth - 1)
+            def _():
+                self.hop_left(z, cut).wait_recv()
+                self.out[rows] += self.line[z, rows].astype(jnp.float32)
+
+        for spot in range(self.depth):
+            self.pair(spot).wait_send()
+
+            @pl.when(z < spot)
+            def _():
+                for cut in range(self.cuts):
+                    self.hop_right(spot, cut).wait_send()
+
+            @pl.when(z > spot)
+            def _():
+                for cut in range(self.cuts):
+                    self.hop_left(spot, cut).wait_send()
+
+
+class RingReduce:
+    def __init__(self, part, work, scratch, where):
+        self.part, self.work, self.where = part, work, where
+        self.from_x, self.from_y, self.x_sent, self.x_recv, self.y_sent, self.y_recv = scratch
+
+    @staticmethod
+    def scratch(*half):
+        return [pltpu.VMEM((3,) + half, jnp.bfloat16)] * 2 + [pltpu.SemaphoreType.DMA((3,))] * 4
+
+    def to_x(self, kind):
+        dp, cp, z, core = self.where
+        source = (
+            self.part(dp ^ 3, 0) if kind == 0 else self.part(dp ^ 1, 0) if kind == 1 else self.work(1)
+        )
+        return send(
+            source, self.from_x.at[kind], self.x_sent.at[kind], self.x_recv.at[kind], (dp ^ 1, cp)
+        )
+
+    def to_y(self, kind):
+        dp, cp, z, core = self.where
+        source = (
+            self.part(dp ^ 3, 1) if kind == 0 else self.part(dp ^ 2, 1) if kind == 1 else self.work(0)
+        )
+        return send(
+            source, self.from_y.at[kind], self.y_sent.at[kind], self.y_recv.at[kind], (dp ^ 2, cp)
+        )
+
+    def start(self):
+        for kind in range(2):
+            self.to_x(kind).start()
+            self.to_y(kind).start()
+
+    def add(self, index, *arrived):
+        target = self.work(index)
+        total = target[...].astype(jnp.float32)
+        for block in arrived:
+            total = total + block[...].astype(jnp.float32)
+        target[...] = total.astype(jnp.bfloat16)
+
+    def middle(self):
+        self.to_x(0).wait_recv()
+        self.add(0, self.from_x.at[0])
+        self.to_y(2).start()
+        self.to_y(0).wait_recv()
+        self.add(1, self.from_y.at[0])
+        self.to_x(2).start()
+
+    def finish(self):
+        for kind in (1, 2):
+            self.to_x(kind).wait_recv()
+            self.to_y(kind).wait_recv()
+        self.add(2, self.from_x.at[1], self.from_y.at[2])
+        self.add(3, self.from_y.at[1], self.from_x.at[2])
+
+    def finish_send(self):
+        for kind in range(3):
+            self.to_x(kind).wait_send()
+            self.to_y(kind).wait_send()
+
+    def places(self):
+        dp = self.where[0]
+        return [(dp ^ 2, 0), (dp ^ 1, 1), (dp, 0), (dp, 1)]
+
+
+def far_first(turn, z, depth):
+    order = []
+    for spot in range(depth):
+        rest = sorted((other for other in range(depth) if other != spot), key=lambda other: (-abs(other - spot), other))
+        ends = [other for other in rest if other in (0, depth - 1)]
+        order.append(ends + [other for other in rest if other not in ends] + [spot])
+    picked = 0
+    for step in range(depth):
+        for spot in range(depth):
+            picked = picked + order[spot][step] * ((turn == step) & (z == spot)).astype(jnp.int32)
+    return picked
+
+
+def near_first(turn, z, depth):
+    picked = 0
+    for step in range(depth):
+        for spot in range(depth):
+            order = sorted(range(depth), key=lambda other: (abs(other - spot), other))
+            picked = picked + order[step] * ((turn == step) & (z == spot)).astype(jnp.int32)
+    return picked
+
+
+def fore_kernel(
     tile,
     tokens_ref,
     gains_ref,
@@ -665,19 +894,21 @@
     input_ref,
     output_ref,
     gateup_ref,
+    down_ref,
     cotangent_own,
     normed_one_out,
-    own_two,
-    cotangent_all,
     input_out,
     output_out,
-    gateup_out,
     raw_out,
     flat_out,
+    forward_out,
+    gateup_out,
     total_out,
     residual_out,
     cosine_ref,
     sine_ref,
+    d_normed_out,
+    down_out,
     input_send,
     output_own,
     gate_send,
@@ -695,6 +926,16 @@
     values,
     flat_send,
     flat_recv,
+    own_two,
+    normed,
+    cotangent,
+    gate_weight,
+    up_weight,
+    down_weight,
+    hidden_up,
+    d_gates,
+    d_ups,
+    down_grad,
     out_sems,
     *sems,
 ):
@@ -737,18 +978,23 @@
     cut_columns(gate_send, 0)
     greet([(dp, cp ^ turn) for turn in range(1, context_count)] + [(dp ^ 1, cp), (dp ^ 2, cp)])
     token_line = LineGather(own_one, normed_one, some(5), where, depth)
-    cotangent_line = LineGather(cotangent_own, cotangent_all, some(5), where, depth)
+    second_line = LineGather(own_two, normed, some(5), where, depth)
+    cotangent_line = LineGather(cotangent_own, cotangent, some(5), where, depth)
     output_line = LineGather(
         output_own, lambda slot: outputs.at[dp, slot // 2, core], some(5), where, depth, False
     )
     input_swap = Swap(input_send, inputs.at[dp], some(3), where, context_count)
     shard = input_send.shape[1]
 
-    def gateup_slot(index):
-        return lambda slot: gateup_out.at[index, dp, pl.ds(pl.multiple_of(slot * shard, 16), shard)]
-
-    gate_swap = Swap(gate_send, gateup_slot(0), some(3), where, context_count)
-    up_swap = Swap(up_send, gateup_slot(1), some(3), where, context_count)
+    each_rows = context_count * shard
+
+    def weight_slot(target):
+        return lambda slot: target.at[
+            pl.ds(pl.multiple_of(dp * each_rows + slot * shard, 16), shard)
+        ]
+
+    gate_swap = Swap(gate_send, weight_slot(gate_weight), some(3), where, context_count)
+    up_swap = Swap(up_send, weight_slot(up_weight), some(3), where, context_count)
     flat_swap = Swap(flat_send, flat_recv, some(3), where, context_count)
     input_ring = RingSpread(
         lambda d: inputs.at[d],
@@ -762,17 +1008,32 @@
         some(2),
         where,
     )
-    half_rows = gateup_out.shape[2] // 2
-
-    def gateup_ring(index):
+    half_rows = each_rows // 2
+
+    def weight_ring(target):
         return RingSpread(
-            lambda d: gateup_out.at[index, d],
-            lambda d, h: gateup_out.at[index, d, pl.ds(h * half_rows, half_rows)],
+            lambda d: target.at[pl.ds(pl.multiple_of(d * each_rows, 16), each_rows)],
+            lambda d, h: target.at[
+                pl.ds(pl.multiple_of(d * each_rows + h * half_rows, 16), half_rows)
+            ],
             some(2),
             where,
         )
 
-    gate_ring, up_ring = gateup_ring(0), gateup_ring(1)
+    gate_ring, up_ring = weight_ring(gate_weight), weight_ring(up_weight)
+    lane_half = width // 2
+
+    def down_part(d, h):
+        return down_grad.at[d, :, pl.ds(h * lane_half, lane_half)]
+
+    down_spread = RingSpread(lambda d: down_grad.at[d], down_part, some(2), where)
+    line = LineScatter(normed_one, d_normed_out, some(8), where, depth)
+
+    def down_work(index):
+        return down_part(*down_ring.places()[index])
+
+    down_ring = RingReduce(down_part, down_work, some(6), where)
+    at_end = (z == 0) | (z == depth - 1)
     share_sent, share_recv = some(2)
 
     def share(mine):
@@ -781,12 +1042,12 @@
 
     input_swap.start()
     gate_swap.start()
+    down_grad[dp] = down_ref[...].astype(jnp.bfloat16)
+    down_spread.start()
     gain_one, gain_two, gain_query, gain_key = split_gains(gains_ref, width)
-    x_float = tokens_ref[...].astype(jnp.float32)
-    hat_one, _ = rms_parts(x_float)
+    hat_one, _ = rms_parts(tokens_ref[...].astype(jnp.float32))
     own_one[...] = (hat_one * gain_one).astype(jnp.bfloat16)
     output_own[...] = output_ref[...].astype(jnp.bfloat16)
-    cut_columns(up_send, half_width)
     place_row, place_column, starts = lay_places(order_ref, lengths_ref, rows, context_count)
     query_place_ref[...] = place_row
     key_place_ref[...] = place_column
@@ -797,20 +1058,24 @@
     )
     cosine_ref[...] = jnp.cos(angles)
     sine_ref[...] = jnp.sin(angles)
+    cut_columns(up_send, half_width)
+    token_line.start()
     input_swap.finish_recv()
     input_ring.start()
     gate_swap.finish_recv()
     gate_ring.start()
+    output_line.start()
+    token_line.step(1)
+    output_line.step(1)
+    input_ring.forward()
+    token_line.step(2)
+    output_line.step(2)
+    token_line.step(3)
+    output_line.step(3)
+    down_spread.forward()
     up_swap.start()
-    input_ring.forward()
-    token_line.start()
-    token_line.step(1)
-    up_swap.finish_recv()
-    up_ring.start()
-    token_line.step(2)
-    gate_ring.forward()
-    output_line.start()
-    token_line.step(3)
+    output_line.finish()
+    output_ring.start()
     token_line.finish()
     input_ring.finish()
     one_copy = pltpu.make_async_copy(normed_one, normed_one_out, out_sems.at[0])
@@ -845,23 +1110,20 @@
         lanes = pl.ds(pl.multiple_of(turn * tile, tile), tile)
         query_place, query_start = query_place_ref[:, lanes], query_start_ref[:, lanes]
 
-        @pl.when(turn == 0)
-        def _():
-            output_line.step(1)
-
         @pl.when(turn == 1)
         def _():
-            output_line.step(2)
-            output_line.step(3)
+            gate_ring.forward()
+            cotangent_line.start()
 
         @pl.when(turn == 2)
         def _():
-            output_line.finish()
-            output_ring.start()
+            output_ring.forward()
 
         @pl.when(turn == 3)
         def _():
-            cotangent_line.start()
+            up_swap.finish_recv()
+            up_ring.start()
+            cotangent_line.step(1)
 
         for head in range(HEADS // KV_HEADS):
             spot = pl.ds(head * HEAD_DIM, HEAD_DIM)
@@ -882,10 +1144,9 @@
 
     lax.fori_loop(0, depth, attend, 0)
     flat_swap.start()
-    output_ring.forward()
-    cotangent_line.step(1)
     output_ring.finish()
     share(True).start()
+    cotangent_line.step(2)
     share(False).wait_recv()
     output_copy = pltpu.make_async_copy(outputs, output_out, out_sems.at[3])
     output_copy.start()
@@ -893,26 +1154,144 @@
     flat_copy = pltpu.make_async_copy(flat_recv, flat_out, out_sems.at[4])
     flat_copy.start()
     flat = flat_recv[...].reshape(HEADS * HEAD_DIM, rows).astype(jnp.float32).T.astype(jnp.bfloat16)
-    residual = x_float + jnp.dot(
+    residual = tokens_ref[...].astype(jnp.float32) + jnp.dot(
         flat, outputs[...].reshape(HEADS * HEAD_DIM, width), preferred_element_type=jnp.float32
     )
     residual_out[...] = residual
     hat_two, _ = rms_parts(residual)
     own_two[...] = (hat_two * gain_two).astype(jnp.bfloat16)
-    cotangent_line.step(2)
+    second_line.start()
+    down_spread.finish()
+
+    def lay_down(step, carry):
+        lanes = pl.ds(pl.multiple_of(step * tile, tile), tile)
+        down_weight[:, lanes] = (
+            down_grad[:, :, lanes]
+            .astype(jnp.float32)
+            .reshape(down_weight.shape[0], tile)
+            .astype(jnp.bfloat16)
+        )
+        return carry
+
+    lax.fori_loop(0, width // tile, lay_down, 0)
     up_ring.forward()
     cotangent_line.step(3)
+    gate_ring.finish()
     cotangent_line.finish()
-    gate_ring.finish()
     up_ring.finish()
+    one_copy.wait()
+    group_rows = context_count * rows
+    parts = normed_one
+
+    def feed(turn, carry):
+        spot = near_first(turn, z, depth)
+        far = jnp.abs(spot - z)
+
+        @pl.when((turn > 0) & (far != jnp.abs(near_first(turn - 1, z, depth) - z)))
+        def _():
+            second_line.step(far)
+
+        @pl.when(turn == 0)
+        def _():
+            second_line.keep().wait()
+
+        second_line.arrive(spot)
+        pair = pl.ds(2 * spot, 2)
+        lanes = pl.ds(pl.multiple_of(spot * tile, tile), tile)
+        block = normed[pair].reshape(tile, width)
+        gate = jnp.dot(block, gate_weight[...], preferred_element_type=jnp.float32)
+        up = jnp.dot(block, up_weight[...], preferred_element_type=jnp.float32)
+        sig = 1.0 / (1.0 + jnp.exp(-gate))
+        act = gate * sig
+        hidden_up[:, lanes] = (act * up).T.astype(jnp.bfloat16)
+        d_hidden = contract_cols(cotangent[pair].reshape(tile, width), down_weight[...])
+        d_gate = (d_hidden * up * (sig * (1.0 + gate * (1.0 - sig)))).astype(jnp.bfloat16)
+        d_up = (d_hidden * act).astype(jnp.bfloat16)
+        d_gates[lanes] = d_gate
+        d_ups[lanes] = d_up
+        part = contract_cols(d_gate, gate_weight[...]) + contract_cols(d_up, up_weight[...])
+        parts[pair] = part.astype(jnp.bfloat16).reshape(2, rows, width)
+        line.pair(spot).start()
+
+        @pl.when(at_end & (turn > 0))
+        def _():
+            line.forward(spot)
+
+        return carry
+
+    lax.fori_loop(0, depth, feed, 0)
+    chunk = 256
+    inner = depth - 1 - z
+    outer = [inner, (depth - 1) * (z // 2 == 0).astype(jnp.int32), (depth - 1) * (z // 2 == 1).astype(jnp.int32)]
+
+    def relay(index):
+        @pl.when(jnp.logical_not(at_end))
+        def _():
+            line.forward(outer[index])
+
+    def down_step(step, carry):
+        lanes = pl.ds(pl.multiple_of(step * chunk, chunk), chunk)
+        right = cotangent[:, :, lanes].reshape(group_rows, chunk)
+        down_grad[:, :, lanes] = (
+            jnp.dot(hidden_up[...], right, preferred_element_type=jnp.float32)
+            .reshape(down_grad.shape[:2] + (chunk,))
+            .astype(jnp.bfloat16)
+        )
+        return carry
+
+    lax.fori_loop(0, width // chunk, down_step, 0)
+    down_ring.start()
+    relay(0)
+
+    def gateup_step(step, carry):
+        lanes = pl.ds(pl.multiple_of(step * chunk, chunk), chunk)
+        left = normed[:, :, lanes].reshape(group_rows, chunk)
+        gate_weight[lanes] = contract_rows(left, d_gates[...]).astype(jnp.bfloat16)
+        up_weight[lanes] = contract_rows(left, d_ups[...]).astype(jnp.bfloat16)
+        return carry
+
+    steps = width // chunk
+    lax.fori_loop(0, steps // 2, gateup_step, 0)
+    relay(1)
+    lax.fori_loop(steps // 2, steps, gateup_step, 0)
+    relay(2)
+    saves = [
+        pltpu.make_async_copy(gate_weight, gateup_out.at[0], out_sems.at[0]),
+        pltpu.make_async_copy(up_weight, gateup_out.at[1], out_sems.at[5]),
+    ]
+    for save in saves:
+        save.start()
+    down_ring.middle()
+
+    second_line.finish(True)
+
+    def forward_step(step, carry):
+        lanes = pl.ds(pl.multiple_of(step * tile, tile), tile)
+        normed[pl.ds(2 * step, 2)] = (
+            contract_rows(hidden_up[:, lanes], down_weight[...])
+            .astype(jnp.bfloat16)
+            .reshape(2, rows, width)
+        )
+        return carry
+
+    lax.fori_loop(0, depth, forward_step, 0)
+    saves.append(pltpu.make_async_copy(normed, forward_out, out_sems.at[6]))
+    saves[2].start()
+    line.finish()
+    down_ring.finish()
+    for half in range(2):
+        down_out[:, pl.ds(half * lane_half, lane_half)] = down_grad[
+            dp, :, pl.ds(half * lane_half, lane_half)
+        ].astype(jnp.float32)
+    down_ring.finish_send()
     share(True).wait_send()
     for swap in (input_swap, gate_swap, up_swap, flat_swap):
         swap.finish_send()
-    for copy in (one_copy, input_copy, raw_copy, output_copy, flat_copy):
+    for copy in (input_copy, raw_copy, output_copy, flat_copy, *saves):
         copy.wait()
 
 
-def front(
+def fore(
     tokens,
     gains,
     order,
@@ -920,6 +1299,7 @@
     attn_input,
     attn_output,
     gate_up,
+    down,
     cotangent,
     data_count,
     context_count,
@@ -936,24 +1316,26 @@
     any_space = pl.BlockSpec(memory_space=pl.ANY)
     in_vmem = pl.BlockSpec(memory_space=pltpu.VMEM)
     in_smem = pl.BlockSpec(memory_space=pltpu.SMEM)
+    down_rows = down.shape[0]
     shapes = [
-        ((context_count, rows, width), bf, any_space),
-        ((rows, width), bf, in_vmem),
         ((context_count, rows, width), bf, any_space),
         ((data_count, context_count, shard, each), bf, any_space),
         ((data_count, depth, 2, shard, width), bf, any_space),
-        ((2, data_count, context_count * shard, hidden), bf, any_space),
         ((each, group_rows), jnp.float32, any_space),
         ((context_count, q_each, rows), bf, any_space),
+        ((context_count, rows, width), bf, any_space),
+        ((2, width, hidden), bf, any_space),
         ((HEADS // KV_HEADS, group_rows), jnp.float32, in_vmem),
         ((rows, width), jnp.float32, in_vmem),
         ((HEAD_DIM // 2, group_rows), jnp.float32, in_vmem),
         ((HEAD_DIM // 2, group_rows), jnp.float32, in_vmem),
+        ((rows, width), jnp.float32, in_vmem),
+        ((down_rows, width), jnp.float32, in_vmem),
     ]
     return pl.pallas_call(
-        functools.partial(front_kernel, 2 * rows),
+        functools.partial(fore_kernel, 2 * rows),
         out_shape=[jax.ShapeDtypeStruct(shape, kind) for shape, kind, _ in shapes],
-        in_specs=[in_vmem] * 2 + [in_smem] * 2 + [in_vmem] * 3 + [any_space],
+        in_specs=[in_vmem] * 2 + [in_smem] * 2 + [in_vmem] * 4 + [any_space],
         out_specs=[space for _, _, space in shapes],
         scratch_shapes=[
             pltpu.VMEM((context_count, shard, each), bf),
@@ -973,449 +1355,29 @@
             pltpu.VMEM((HEAD_DIM, group_rows), bf),
             pltpu.VMEM((context_count, q_each, rows), bf),
             pltpu.VMEM((context_count, q_each, rows), bf),
-            pltpu.SemaphoreType.DMA((6,)),
-        ]
-        + LineGather.scratch(depth) * 3
-        + Swap.scratch(context_count) * 4
-        + RingSpread.scratch() * 4
-        + [pltpu.SemaphoreType.DMA] * 2,
-        compiler_params=pltpu.CompilerParams(
-            collective_id=0, has_side_effects=True, vmem_limit_bytes=56 * 2**20
-        ),
-        name="front",
-    )(tokens, gains, order, lengths, attn_input, attn_output, gate_up, cotangent)
-
-
-class LineScatter:
-    cuts = 2
-
-    def __init__(self, part_ref, out_ref, scratch, where, depth):
-        self.part, self.out, self.where, self.depth = part_ref, out_ref, where, depth
-        self.sib, self.line = scratch[:2]
-        (
-            self.sib_sent,
-            self.sib_recv,
-            self.right_sent,
-            self.right_recv,
-            self.left_sent,
-            self.left_recv,
-        ) = scratch[2:]
-        self.size = part_ref.shape[1] // self.cuts
-
-    @classmethod
-    def scratch(cls, depth, rows, width):
-        return [
-            pltpu.VMEM((depth, rows, width), jnp.bfloat16),
-            pltpu.VMEM((depth + 1, rows, width), jnp.bfloat16),
-        ] + [pltpu.SemaphoreType.DMA((depth,))] * 2 + [
-            pltpu.SemaphoreType.DMA((depth * cls.cuts,))
-        ] * 4
-
-    def pair(self, spot):
-        dp, cp, z, core = self.where
-        return send(
-            self.part.at[2 * spot + 1 - core],
-            self.sib.at[spot],
-            self.sib_sent.at[spot],
-            self.sib_recv.at[spot],
-            (dp, cp ^ 1),
-        )
-
-    def rows(self, cut):
-        return pl.ds(cut * self.size, self.size)
-
-    def hop_right(self, spot, cut):
-        dp, cp, z, core = self.where
-        index = spot * self.cuts + cut
-        return send(
-            self.part.at[2 * spot + core, self.rows(cut)],
-            self.line.at[spot + 1, self.rows(cut)],
-            self.right_sent.at[index],
-            self.right_recv.at[index],
-            (dp, cp + 2),
-        )
-
-    def hop_left(self, spot, cut):
-        dp, cp, z, core = self.where
-        index = spot * self.cuts + cut
-        return send(
-            self.part.at[2 * spot + core, self.rows(cut)],
-            self.line.at[spot, self.rows(cut)],
-            self.left_sent.at[index],
-            self.left_recv.at[index],
-            (dp, cp - 2),
-        )
-
-    def order(self):
-        spots = []
-        for turn in range(self.depth):
-            spots += [self.depth - 1 - turn, turn]
-        return list(dict.fromkeys(spots))
-
-    def chip_sum(self, spot, cut):
-        rows = self.rows(cut)
-        mine = self.part[2 * spot + self.where[3], rows].astype(jnp.float32)
-        return mine + self.sib[spot, rows].astype(jnp.float32)
-
-    def pass_on(self, spot, cut, arrived, slot, hop):
-        total = self.chip_sum(spot, cut)
-        if arrived is not None:
-            arrived.wait_recv()
-            total = total + self.line[slot, self.rows(cut)].astype(jnp.float32)
-        self.part[2 * spot + self.where[3], self.rows(cut)] = total.astype(jnp.bfloat16)
-        hop.start()
-
-    def forward(self, spot, cuts=None):
-        z, core = self.where[2], self.where[3]
-        cuts = range(self.cuts) if cuts is None else cuts
-        if 0 in cuts:
-
-            @pl.when(z != spot)
-            def _():
-                self.pair(spot).wait_recv()
-
-        for cut in cuts:
-            right, left = self.hop_right(spot, cut), self.hop_left(spot, cut)
-
-            @pl.when((z < spot) & (z > 0))
-            def _():
-                self.pass_on(spot, cut, right, spot + 1, right)
-
-            @pl.when((z < spot) & (z == 0))
-            def _():
-                self.pass_on(spot, cut, None, None, right)
-
-            @pl.when((z > spot) & (z < self.depth - 1))
-            def _():
-                self.pass_on(spot, cut, left, spot, left)
-
-            @pl.when((z > spot) & (z == self.depth - 1))
-            def _():
-                self.pass_on(spot, cut, None, None, left)
-
-    def finish(self):
-        z = self.where[2]
-        self.pair(z).wait_recv()
-        for cut in range(self.cuts):
-            rows = self.rows(cut)
-            self.out[rows] = self.chip_sum(z, cut)
-
-            @pl.when(z > 0)
-            def _():
-                self.hop_right(z, cut).wait_recv()
-                self.out[rows] += self.line[z + 1, rows].astype(jnp.float32)
-
-            @pl.when(z < self.depth - 1)
-            def _():
-                self.hop_left(z, cut).wait_recv()
-                self.out[rows] += self.line[z, rows].astype(jnp.float32)
-
-        for spot in range(self.depth):
-            self.pair(spot).wait_send()
-
-            @pl.when(z < spot)
-            def _():
-                for cut in range(self.cuts):
-                    self.hop_right(spot, cut).wait_send()
-
-            @pl.when(z > spot)
-            def _():
-                for cut in range(self.cuts):
-                    self.hop_left(spot, cut).wait_send()
-
-
-class RingReduce:
-    def __init__(self, part, work, scratch, where):
-        self.part, self.work, self.where = part, work, where
-        self.from_x, self.from_y, self.x_sent, self.x_recv, self.y_sent, self.y_recv = scratch
-
-    @staticmethod
-    def scratch(*half):
-        return [pltpu.VMEM((3,) + half, jnp.bfloat16)] * 2 + [pltpu.SemaphoreType.DMA((3,))] * 4
-
-    def to_x(self, kind):
-        dp, cp, z, core = self.where
-        source = (
-            self.part(dp ^ 3, 0) if kind == 0 else self.part(dp ^ 1, 0) if kind == 1 else self.work(1)
-        )
-        return send(
-            source, self.from_x.at[kind], self.x_sent.at[kind], self.x_recv.at[kind], (dp ^ 1, cp)
-        )
-
-    def to_y(self, kind):
-        dp, cp, z, core = self.where
-        source = (
-            self.part(dp ^ 3, 1) if kind == 0 else self.part(dp ^ 2, 1) if kind == 1 else self.work(0)
-        )
-        return send(
-            source, self.from_y.at[kind], self.y_sent.at[kind], self.y_recv.at[kind], (dp ^ 2, cp)
-        )
-
-    def start(self):
-        for kind in range(2):
-            self.to_x(kind).start()
-            self.to_y(kind).start()
-
-    def add(self, index, *arrived):
-        target = self.work(index)
-        total = target[...].astype(jnp.float32)
-        for block in arrived:
-            total = total + block[...].astype(jnp.float32)
-        target[...] = total.astype(jnp.bfloat16)
-
-    def middle(self):
-        self.to_x(0).wait_recv()
-        self.add(0, self.from_x.at[0])
-        self.to_y(2).start()
-        self.to_y(0).wait_recv()
-        self.add(1, self.from_y.at[0])
-        self.to_x(2).start()
-
-    def finish(self):
-        for kind in (1, 2):
-            self.to_x(kind).wait_recv()
-            self.to_y(kind).wait_recv()
-        self.add(2, self.from_x.at[1], self.from_y.at[2])
-        self.add(3, self.from_y.at[1], self.from_x.at[2])
-
-    def finish_send(self):
-        for kind in range(3):
-            self.to_x(kind).wait_send()
-            self.to_y(kind).wait_send()
-
-    def places(self):
-        dp = self.where[0]
-        return [(dp ^ 2, 0), (dp ^ 1, 1), (dp, 0), (dp, 1)]
-
-
-def far_first(turn, z, depth):
-    order = []
-    for spot in range(depth):
-        rest = sorted((other for other in range(depth) if other != spot), key=lambda other: (-abs(other - spot), other))
-        ends = [other for other in rest if other in (0, depth - 1)]
-        order.append(ends + [other for other in rest if other not in ends] + [spot])
-    picked = 0
-    for step in range(depth):
-        for spot in range(depth):
-            picked = picked + order[spot][step] * ((turn == step) & (z == spot)).astype(jnp.int32)
-    return picked
-
-
-def near_first(turn, z, depth):
-    picked = 0
-    for step in range(depth):
-        for spot in range(depth):
-            order = sorted(range(depth), key=lambda other: (abs(other - spot), other))
-            picked = picked + order[step] * ((turn == step) & (z == spot)).astype(jnp.int32)
-    return picked
-
-
-def middle_kernel(
-    own_ref,
-    cotangent_in,
-    gateup_in,
-    down_in,
-    d_normed_out,
-    forward_out,
-    down_out,
-    gateup_out,
-    normed,
-    cotangent,
-    gate_weight,
-    up_weight,
-    down_weight,
-    hidden_up,
-    d_gates,
-    d_ups,
-    parts,
-    forwards,
-    down_grad,
-    gateup_grad,
-    load_sems,
-    save_sems,
-    *scratch,
-):
-    where = place()
-    dp, cp, z, core = where
-    count, rows, width = normed.shape
-    depth = count // 2
-    tile = 2 * rows
-    group_rows = count * rows
-    loads = [
-        pltpu.make_async_copy(source, target, load_sems.at[index])
-        for index, (source, target) in enumerate(
-            [
-                (gateup_in.at[0], gate_weight),
-                (gateup_in.at[1], up_weight),
-                (cotangent_in, cotangent),
-                (down_in, down_weight),
-            ]
-        )
-    ]
-    greet(
-        [(dp, cp ^ turn) for turn in range(1, count)]
-        + [(dp ^ 1, cp), (dp ^ 2, cp)]
-    )
-    second_line = LineGather(own_ref, normed, scratch[:5], where, depth)
-    line = LineScatter(parts, d_normed_out, scratch[5:13], where, depth)
-    lane_half = width // 2
-
-    def down_part(d, h):
-        return down_grad.at[d, :, pl.ds(h * lane_half, lane_half)]
-
-    def down_work(index):
-        return down_part(*down_ring.places()[index])
-
-    down_ring = RingReduce(down_part, down_work, scratch[13:], where)
-    second_line.start()
-    for load in loads:
-        load.start()
-    at_end = (z == 0) | (z == depth - 1)
-    for load in loads:
-        load.wait()
-
-    def feed(turn, carry):
-        spot = near_first(turn, z, depth)
-        far = jnp.abs(spot - z)
-
-        @pl.when((turn > 0) & (far != jnp.abs(near_first(turn - 1, z, depth) - z)))
-        def _():
-            second_line.step(far)
-
-        @pl.when(turn == 0)
-        def _():
-            second_line.keep().wait()
-
-        second_line.arrive(spot)
-        pair = pl.ds(2 * spot, 2)
-        lanes = pl.ds(pl.multiple_of(spot * tile, tile), tile)
-        block = normed[pair].reshape(tile, width)
-        gate = jnp.dot(block, gate_weight[...], preferred_element_type=jnp.float32)
-        up = jnp.dot(block, up_weight[...], preferred_element_type=jnp.float32)
-        sig = 1.0 / (1.0 + jnp.exp(-gate))
-        act = gate * sig
-        hidden_up[:, lanes] = (act * up).T.astype(jnp.bfloat16)
-        d_hidden = contract_cols(cotangent[pair].reshape(tile, width), down_weight[...])
-        d_gate = (d_hidden * up * (sig * (1.0 + gate * (1.0 - sig)))).astype(jnp.bfloat16)
-        d_up = (d_hidden * act).astype(jnp.bfloat16)
-        d_gates[lanes] = d_gate
-        d_ups[lanes] = d_up
-        part = contract_cols(d_gate, gate_weight[...]) + contract_cols(d_up, up_weight[...])
-        parts[pair] = part.astype(jnp.bfloat16).reshape(2, rows, width)
-        line.pair(spot).start()
-
-        @pl.when(at_end & (turn > 0))
-        def _():
-            line.forward(spot)
-
-        return carry
-
-    lax.fori_loop(0, depth, feed, 0)
-    chunk = 256
-    inner = depth - 1 - z
-    outer = [inner, (depth - 1) * (z // 2 == 0).astype(jnp.int32), (depth - 1) * (z // 2 == 1).astype(jnp.int32)]
-
-    def relay(index):
-        @pl.when(jnp.logical_not(at_end))
-        def _():
-            line.forward(outer[index])
-
-    def down_step(step, carry):
-        lanes = pl.ds(pl.multiple_of(step * chunk, chunk), chunk)
-        right = cotangent[:, :, lanes].reshape(group_rows, chunk)
-        down_grad[:, :, lanes] = (
-            jnp.dot(hidden_up[...], right, preferred_element_type=jnp.float32)
-            .reshape(down_grad.shape[:2] + (chunk,))
-            .astype(jnp.bfloat16)
-        )
-        return carry
-
-    lax.fori_loop(0, width // chunk, down_step, 0)
-    down_ring.start()
-    relay(0)
-
-    def gateup_step(step, carry):
-        lanes = pl.ds(pl.multiple_of(step * chunk, chunk), chunk)
-        left = normed[:, :, lanes].reshape(group_rows, chunk)
-        gateup_grad[0, lanes] = contract_rows(left, d_gates[...]).astype(jnp.bfloat16)
-        gateup_grad[1, lanes] = contract_rows(left, d_ups[...]).astype(jnp.bfloat16)
-        return carry
-
-    steps = width // chunk
-    lax.fori_loop(0, steps // 2, gateup_step, 0)
-    relay(1)
-    lax.fori_loop(steps // 2, steps, gateup_step, 0)
-    relay(2)
-    saves = [pltpu.make_async_copy(gateup_grad, gateup_out, save_sems.at[0])]
-    saves[0].start()
-    down_ring.middle()
-
-    def forward_step(step, carry):
-        lanes = pl.ds(pl.multiple_of(step * tile, tile), tile)
-        forwards[pl.ds(2 * step, 2)] = (
-            contract_rows(hidden_up[:, lanes], down_weight[...])
-            .astype(jnp.bfloat16)
-            .reshape(2, rows, width)
-        )
-        return carry
-
-    lax.fori_loop(0, depth, forward_step, 0)
-    saves.append(pltpu.make_async_copy(forwards, forward_out, save_sems.at[1]))
-    saves[1].start()
-    line.finish()
-    second_line.finish(True)
-    down_ring.finish()
-    for half in range(2):
-        down_out[:, pl.ds(half * lane_half, lane_half)] = down_grad[
-            dp, :, pl.ds(half * lane_half, lane_half)
-        ].astype(jnp.float32)
-    down_ring.finish_send()
-    for save in saves:
-        save.wait()
-
-
-def middle(own, cotangent, gateup, down, data_count, collective_id):
-    count, rows, width = cotangent.shape
-    depth = count // 2
-    hidden = down.shape[0]
-    group_rows = count * rows
-    bf = jnp.bfloat16
-    any_space = pl.BlockSpec(memory_space=pl.ANY)
-    in_vmem = pl.BlockSpec(memory_space=pltpu.VMEM)
-    return pl.pallas_call(
-        middle_kernel,
-        out_shape=[
-            jax.ShapeDtypeStruct((rows, width), jnp.float32),
-            jax.ShapeDtypeStruct((count, rows, width), bf),
-            jax.ShapeDtypeStruct((hidden // data_count, width), jnp.float32),
-            jax.ShapeDtypeStruct((2, width, hidden), bf),
-        ],
-        in_specs=[in_vmem] + [any_space] * 3,
-        out_specs=[in_vmem, any_space, in_vmem, any_space],
-        scratch_shapes=[
-            pltpu.VMEM((count, rows, width), bf),
-            pltpu.VMEM((count, rows, width), bf),
+            pltpu.VMEM((rows, width), bf),
+            pltpu.VMEM((context_count, rows, width), bf),
+            pltpu.VMEM((context_count, rows, width), bf),
             pltpu.VMEM((width, hidden), bf),
             pltpu.VMEM((width, hidden), bf),
             pltpu.VMEM((hidden, width), bf),
             pltpu.VMEM((hidden, group_rows), bf),
             pltpu.VMEM((group_rows, hidden), bf),
             pltpu.VMEM((group_rows, hidden), bf),
-            pltpu.VMEM((count, rows, width), bf),
-            pltpu.VMEM((count, rows, width), bf),
-            pltpu.VMEM((data_count, hidden // data_count, width), bf),
-            pltpu.VMEM((2, width, hidden), bf),
-            pltpu.SemaphoreType.DMA((4,)),
-            pltpu.SemaphoreType.DMA((2,)),
+            pltpu.VMEM((data_count, down_rows, width), bf),
+            pltpu.SemaphoreType.DMA((7,)),
         ]
-        + LineGather.scratch(depth)
+        + LineGather.scratch(depth) * 4
+        + Swap.scratch(context_count) * 4
+        + RingSpread.scratch() * 5
         + LineScatter.scratch(depth, rows, width)
-        + RingReduce.scratch(hidden // data_count, width // 2),
+        + RingReduce.scratch(down_rows, width // 2)
+        + [pltpu.SemaphoreType.DMA] * 2,
         compiler_params=pltpu.CompilerParams(
-            collective_id=collective_id, has_side_effects=True, vmem_limit_bytes=60 * 2**20
+            collective_id=0, has_side_effects=True, vmem_limit_bytes=63 * 2**20
         ),
-        name="middle",
-    )(own, cotangent, gateup, down)
+        name="fore",
+    )(tokens, gains, order, lengths, attn_input, attn_output, gate_up, down, cotangent)
 
 
 def back_kernel(
@@ -1824,7 +1786,10 @@
         )
         copy.wait_recv()
         copy.wait_send()
-    gains_out[...] = jnp.sum(all_gains[...], axis=0)
+    gain_total = jnp.sum(all_gains[...], axis=0)
+    lanes = gains_out.shape[1]
+    for line in range(gains_out.shape[0]):
+        gains_out[line : line + 1] = gain_total[:, line * lanes : (line + 1) * lanes]
     total = outputs[dp, z, core].astype(jnp.float32)
     for far in range(1, depth):
         output_hop(far, False).wait_recv()
@@ -1879,7 +1844,7 @@
         out_shape=[
             jax.ShapeDtypeStruct((rows, width), bf),
             jax.ShapeDtypeStruct((rows, width), f32),
-            jax.ShapeDtypeStruct((1, gain_width), f32),
+            jax.ShapeDtypeStruct(gains.shape, f32),
             jax.ShapeDtypeStruct((shard, width), f32),
             jax.ShapeDtypeStruct((count, shard, each), bf),
             jax.ShapeDtypeStruct((2, count, shard, hidden), bf),
@@ -2012,7 +1977,7 @@
     def rows_of(array):
         axis = array.ndim - 2
         shape = list(array.shape)
-        if shape[axis] > 1:
+        if shape[axis] % (8 * parts) == 0:
             shape[axis] //= parts
             return pl.BlockSpec(
                 tuple(shape), lambda step: tuple(step if d == axis else 0 for d in range(len(shape)))
@@ -2059,48 +2024,40 @@
 ):
     context_count = lax.axis_size("cp")
     data_count = lax.axis_size("dp")
-    model_width = tokens.shape[1]
-    gains_row = norm_gains.reshape(1, -1)
-    down_part = lax.all_gather(down_weight.astype(jnp.bfloat16), "dp", axis=0, tiled=True)
+    gain_lines = norm_gains.reshape(-1, 2 * HEAD_DIM)
     (
         normed_one,
-        own_two,
-        cotangent_all,
         input_part,
         output_all,
-        gateup_part,
         raw,
         flat_parts,
+        forward_parts,
+        gateup_grad,
         log_total,
         residual,
         cosine,
         sine,
-    ) = front(
+        d_normed_two,
+        grad_down,
+    ) = fore(
         tokens,
-        gains_row,
+        gain_lines,
         block_order,
         sequence_lengths,
         attn_input,
         attn_output,
         gate_up,
+        down_weight,
         output_cotangent,
         data_count,
         context_count,
-    )
-    d_normed_two, forward_parts, grad_down, gateup_grad = middle(
-        own_two,
-        cotangent_all,
-        gateup_part.reshape(2, model_width, -1),
-        down_part,
-        data_count,
-        3,
     )
     mixed, token_gradient, grad_gains, grad_output, grad_input, grad_gateup = back(
         tokens,
         output_cotangent,
         residual,
         d_normed_two,
-        gains_row,
+        gain_lines,
         block_order,
         sequence_lengths,
         cosine,
@@ -2128,9 +2085,9 @@
         down_weight,
         down_moment,
         down_square,
-        gains_row,
-        gains_moment.reshape(1, -1),
-        gains_square.reshape(1, -1),
+        gain_lines,
+        gains_moment.reshape(gain_lines.shape),
+        gains_square.reshape(gain_lines.shape),
     )
     results = update(
         grad_gateup, grad_input, grad_output, grad_down, grad_gains, states, data_count

time: 346 us -> 313 us (0.905)
  between operations: 14.1 us -> 0.7 us
  Pallas kernels: 322 us -> 311 us
  other arithmetic: 6.28 us -> 0 us
    pallas_call x2 -> x1, Pallas kernels: 195 us -> 183 us  [fore(): pl.pallas_call(functools.partial(fore_kernel, 2 * rows), out_shape=[jax.S...]
    pallas_call x3 -> x0, other arithmetic: 4.05 us -> none  [update(): pl.pallas_call(functools.partial(update_kernel, data_count), grid=(parts,...]
  transfers between devices with their start and end apart: 1 -> 0, of which waited for: 0 -> 0; matrix products, arithmetic and copies ran while one was open for 1% -> 0% of each run, Pallas kernels for 36% -> 0%
where the time goes in v1:
time: 313 us
  Pallas kernels  311 us (99%)
    pallas_call x1, Pallas kernels, fore(): pl.pallas_call(functools.partial(fore_kernel, 2 * rows), out_shape=[jax.S...  183 us
    pallas_call x1, Pallas kernels, back(): pl.pallas_call(back_kernel, out_shape=[jax.ShapeDtypeStruct((rows, width)...  114 us
    pallas_call x1, Pallas kernels, update(): pl.pallas_call(functools.partial(update_kernel, data_count), grid=(parts,...  13.2 us

profile of v1, /device:TPU:0, one launch (start us, length us, event | category | flops | bytes accessed | tf_op | source)
XLA Modules:
  0.0 312.9 jit_solution(14885752460901826104)
XLA Ops:
  0.7 183.0 %fore.1 = (bf16[8,128,1536]{2,1,0:T(8,128)(2,1)}, bf16[4,8,48,320]{3,2,1,0:T(8,128)(2,1)}, bf16[4,4,2,48,1536]{4,3,2,1,0:T(8,128)(2,1)}, f32[320,1024]{1,0:T(8,1...) custom-call(bf16[128,1536]{1,0:T(8,128)(2,1)} %tokens_ref.3, ...), custom_call_target="tpu_custom_call" | custom-call | tf_op jit(solution)/shard_map/fore/pallas_call | solution.py:1335
  183.6 114.4 %back.1 = (bf16[128,1536]{1,0:T(8,128)(2,1)}, f32[128,1536]{1,0:T(8,128)}, f32[25,128]{1,0:T(8,128)}, f32[48,1536]{1,0:T(8,128)}, bf16[8,48,320]{2,1,0:T(8,128)(2,1)}, /*index=5*/bf16[2,8,48,864]{3,2,1,0:T(8,128)(2,1)}) custom-call(bf16[128,1536]{1,0:T(8,128)(2,1)} %tokens_ref.3, bf16[128,1536]{1,0:T(8,128)(2,1)} %cotangent_ref.1, ...), custom_call_target="tpu_custom_call" | custom-call | tf_op jit(solution)/shard_map/back/pallas_call | solution.py:1842
  298.0 0.0 copy-start.1
  298.0 0.0 copy-start
  298.0 13.2 %update.1 = (f32[48,2560]{1,0:T(8,128)}, f32[48,2560]{1,0:T(8,128)}, f32[48,2560]{1,0:T(8,128)}, f32[48,1536]{1,0:T(8,128)}, f32[48,1536]{1,0:T(8,128)}, /*index...) custom-call(bf16[2,8,48,864]{3,2,1,0:T(8,128)(2,1)} %get-tuple-eleme, ...), custom_call_target="tpu_custom_call" | custom-call | tf_op jit(solution)/shard_map/update/pallas_call | solution.py:1989
  311.3 0.0 copy-done.1
  311.3 0.7 copy.38
  312.1 0.0 copy-done
  312.1 0.9 copy.39
Async XLA Ops:
  298.0 13.3 %copy-start.1 = (bf16[128,1536]{1,0:T(8,128)(2,1)S(1)}, bf16[128,1536]{1,0:T(8,128)(2,1)}, u32[]{:S(2)}) copy-start(bf16[128,1536]{1,0:T(8,128)(2,1)} %get-tuple-element.102) | copy-start | bytes 1179652
  298.0 14.0 %copy-start = (f32[128,1536]{1,0:T(8,128)S(1)}, f32[128,1536]{1,0:T(8,128)}, u32[]{:S(2)}) copy-start(f32[128,1536]{1,0:T(8,128)} %get-tuple-element.103) | copy-start | bytes 2359300

commit v2 on v1

--- a/solution.py
+++ b/solution.py
@@ -520,6 +520,44 @@
             @pl.when((spot >= z) & (z > 0))
             def _():
                 self.copy("left", slot, self.own).wait_send()
+
+
+class HalvedGather:
+    def __init__(self, own_ref, all_ref, sems, where, depth):
+        half = own_ref.shape[0] // 2
+        count = len(sems) // 2
+
+        def line(index):
+            rows = pl.ds(index * half, half)
+            return LineGather(
+                own_ref.at[rows],
+                lambda slot: all_ref.at[slot, rows],
+                sems[index * count : (index + 1) * count],
+                where,
+                depth,
+            )
+
+        self.lines = [line(0), line(1)]
+
+    def start(self):
+        for line in self.lines:
+            line.start()
+
+    def step(self, far):
+        for line in self.lines:
+            line.step(far)
+
+    def arrive(self, spot):
+        for line in self.lines:
+            line.arrive(spot)
+
+    def keep_wait(self):
+        for line in self.lines:
+            line.keep().wait()
+
+    def finish(self, arrived=False):
+        for line in self.lines:
+            line.finish(arrived)
 
 
 class Swap:
@@ -977,8 +1015,8 @@
 
     cut_columns(gate_send, 0)
     greet([(dp, cp ^ turn) for turn in range(1, context_count)] + [(dp ^ 1, cp), (dp ^ 2, cp)])
-    token_line = LineGather(own_one, normed_one, some(5), where, depth)
-    second_line = LineGather(own_two, normed, some(5), where, depth)
+    token_line = HalvedGather(own_one, normed_one, some(10), where, depth)
+    second_line = HalvedGather(own_two, normed, some(10), where, depth)
     cotangent_line = LineGather(cotangent_own, cotangent, some(5), where, depth)
     output_line = LineGather(
         output_own, lambda slot: outputs.at[dp, slot // 2, core], some(5), where, depth, False
@@ -1193,7 +1231,7 @@
 
         @pl.when(turn == 0)
         def _():
-            second_line.keep().wait()
+            second_line.keep_wait()
 
         second_line.arrive(spot)
         pair = pl.ds(2 * spot, 2)
@@ -1367,7 +1405,7 @@
             pltpu.VMEM((data_count, down_rows, width), bf),
             pltpu.SemaphoreType.DMA((7,)),
         ]
-        + LineGather.scratch(depth) * 4
+        + LineGather.scratch(depth) * 6
         + Swap.scratch(context_count) * 4
         + RingSpread.scratch() * 5
         + LineScatter.scratch(depth, rows, width)
@@ -1742,9 +1780,6 @@
     def _():
         first_line.forward(far_first(2, z, depth))
 
-    output_ring.finish()
-    for far in range(depth - 1, 0, -1):
-        output_hop(far, True).start()
     input_ring.finish()
     input_swap.start()
     first_line.finish()
@@ -1756,6 +1791,9 @@
         send(
             own_gains, line_gains.at[cp], line_sent.at[turn], line_recv.at[turn], (dp, cp ^ turn)
         ).start()
+    output_ring.finish()
+    for far in range(depth - 1, 0, -1):
+        output_hop(far, True).start()
     token_out[...] = d_residual[...] + norm_back(d_one * gain_one, hat_one, inv_one)
     for turn in range(1, count):
         copy = send(

time: 313 us -> 308 us (0.984)
  Pallas kernels: 311 us -> 306 us
    pallas_call x1, Pallas kernels: 114 us -> 111 us  [back(): pl.pallas_call(back_kernel, out_shape=[jax.ShapeDtypeStruct((rows, width)...]
where the time goes in v2:
time: 308 us
  Pallas kernels  306 us (99%)
    pallas_call x1, Pallas kernels, fore(): pl.pallas_call(functools.partial(fore_kernel, 2 * rows), out_shape=[jax.S...  181 us
    pallas_call x1, Pallas kernels, back(): pl.pallas_call(back_kernel, out_shape=[jax.ShapeDtypeStruct((rows, width)...  111 us
    pallas_call x1, Pallas kernels, update(): pl.pallas_call(functools.partial(update_kernel, data_count), grid=(parts,...  13.2 us

profile of v2, /device:TPU:0, one launch (start us, length us, event | category | flops | bytes accessed | tf_op | source)
XLA Modules:
  0.0 308.2 jit_solution(3121253065143845164)
XLA Ops:
  0.7 181.4 %fore.1 = (bf16[8,128,1536]{2,1,0:T(8,128)(2,1)}, bf16[4,8,48,320]{3,2,1,0:T(8,128)(2,1)}, bf16[4,4,2,48,1536]{4,3,2,1,0:T(8,128)(2,1)}, f32[320,1024]{1,0:T(8,1...) custom-call(bf16[128,1536]{1,0:T(8,128)(2,1)} %tokens_ref.3, ...), custom_call_target="tpu_custom_call" | custom-call | tf_op jit(solution)/shard_map/fore/pallas_call | solution.py:1373
  182.1 111.2 %back.1 = (bf16[128,1536]{1,0:T(8,128)(2,1)}, f32[128,1536]{1,0:T(8,128)}, f32[25,128]{1,0:T(8,128)}, f32[48,1536]{1,0:T(8,128)}, bf16[8,48,320]{2,1,0:T(8,128)(2,1)}, /*index=5*/bf16[2,8,48,864]{3,2,1,0:T(8,128)(2,1)}) custom-call(bf16[128,1536]{1,0:T(8,128)(2,1)} %tokens_ref.3, bf16[128,1536]{1,0:T(8,128)(2,1)} %cotangent_ref.1, ...), custom_call_target="tpu_custom_call" | custom-call | tf_op jit(solution)/shard_map/back/pallas_call | solution.py:1880
  293.3 0.0 copy-start.1
  293.3 0.0 copy-start
  293.3 13.2 %update.1 = (f32[48,2560]{1,0:T(8,128)}, f32[48,2560]{1,0:T(8,128)}, f32[48,2560]{1,0:T(8,128)}, f32[48,1536]{1,0:T(8,128)}, f32[48,1536]{1,0:T(8,128)}, /*index...) custom-call(bf16[2,8,48,864]{3,2,1,0:T(8,128)(2,1)} %get-tuple-eleme, ...), custom_call_target="tpu_custom_call" | custom-call | tf_op jit(solution)/shard_map/update/pallas_call | solution.py:2027
  306.6 0.0 copy-done.1
  306.6 0.7 copy.38
  307.3 0.0 copy-done
  307.3 0.9 copy.39
Async XLA Ops:
  293.3 13.3 %copy-start.1 = (bf16[128,1536]{1,0:T(8,128)(2,1)S(1)}, bf16[128,1536]{1,0:T(8,128)(2,1)}, u32[]{:S(2)}) copy-start(bf16[128,1536]{1,0:T(8,128)(2,1)} %get-tuple-element.102) | copy-start | bytes 1179652
  293.3 14.0 %copy-start = (f32[128,1536]{1,0:T(8,128)S(1)}, f32[128,1536]{1,0:T(8,128)}, u32[]{:S(2)}) copy-start(f32[128,1536]{1,0:T(8,128)} %get-tuple-element.103) | copy-start | bytes 2359300

commit v3 on v2

--- a/solution.py
+++ b/solution.py
@@ -1212,8 +1212,8 @@
         return carry
 
     lax.fori_loop(0, width // tile, lay_down, 0)
+    cotangent_line.step(3)
     up_ring.forward()
-    cotangent_line.step(3)
     gate_ring.finish()
     cotangent_line.finish()
     up_ring.finish()
@@ -1792,7 +1792,7 @@
             own_gains, line_gains.at[cp], line_sent.at[turn], line_recv.at[turn], (dp, cp ^ turn)
         ).start()
     output_ring.finish()
-    for far in range(depth - 1, 0, -1):
+    for far in range(1, depth):
         output_hop(far, True).start()
     token_out[...] = d_residual[...] + norm_back(d_one * gain_one, hat_one, inv_one)
     for turn in range(1, count):

time: 308 us -> 307 us (level)
  no operation moved by 1% of the time
where the time goes in v3:
time: 307 us
  Pallas kernels  304 us (99%)
    pallas_call x1, Pallas kernels, fore(): pl.pallas_call(functools.partial(fore_kernel, 2 * rows), out_shape=[jax.S...  181 us
    pallas_call x1, Pallas kernels, back(): pl.pallas_call(back_kernel, out_shape=[jax.ShapeDtypeStruct((rows, width)...  110 us
    pallas_call x1, Pallas kernels, update(): pl.pallas_call(functools.partial(update_kernel, data_count), grid=(parts,...  13.2 us

profile of v3, /device:TPU:0, one launch (start us, length us, event | category | flops | bytes accessed | tf_op | source)
XLA Modules:
  0.0 306.6 jit_solution(12453173975739715903)
XLA Ops:
  0.7 181.4 %fore.1 = (bf16[8,128,1536]{2,1,0:T(8,128)(2,1)}, bf16[4,8,48,320]{3,2,1,0:T(8,128)(2,1)}, bf16[4,4,2,48,1536]{4,3,2,1,0:T(8,128)(2,1)}, f32[320,1024]{1,0:T(8,1...) custom-call(bf16[128,1536]{1,0:T(8,128)(2,1)} %tokens_ref.3, ...), custom_call_target="tpu_custom_call" | custom-call | tf_op jit(solution)/shard_map/fore/pallas_call | solution.py:1373
  182.1 109.6 %back.1 = (bf16[128,1536]{1,0:T(8,128)(2,1)}, f32[128,1536]{1,0:T(8,128)}, f32[25,128]{1,0:T(8,128)}, f32[48,1536]{1,0:T(8,128)}, bf16[8,48,320]{2,1,0:T(8,128)(2,1)}, /*index=5*/bf16[2,8,48,864]{3,2,1,0:T(8,128)(2,1)}) custom-call(bf16[128,1536]{1,0:T(8,128)(2,1)} %tokens_ref.3, bf16[128,1536]{1,0:T(8,128)(2,1)} %cotangent_ref.1, ...), custom_call_target="tpu_custom_call" | custom-call | tf_op jit(solution)/shard_map/back/pallas_call | solution.py:1880
  291.7 0.0 copy-start.1
  291.7 0.0 copy-start
  291.7 13.2 %update.1 = (f32[48,2560]{1,0:T(8,128)}, f32[48,2560]{1,0:T(8,128)}, f32[48,2560]{1,0:T(8,128)}, f32[48,1536]{1,0:T(8,128)}, f32[48,1536]{1,0:T(8,128)}, /*index...) custom-call(bf16[2,8,48,864]{3,2,1,0:T(8,128)(2,1)} %get-tuple-eleme, ...), custom_call_target="tpu_custom_call" | custom-call | tf_op jit(solution)/shard_map/update/pallas_call | solution.py:2027
  304.9 0.0 copy-done.1
  304.9 0.7 copy.38
  305.7 0.0 copy-done
  305.7 0.9 copy.39
Async XLA Ops:
  291.7 13.3 %copy-start.1 = (bf16[128,1536]{1,0:T(8,128)(2,1)S(1)}, bf16[128,1536]{1,0:T(8,128)(2,1)}, u32[]{:S(2)}) copy-start(bf16[128,1536]{1,0:T(8,128)(2,1)} %get-tuple-element.102) | copy-start | bytes 1179652
  291.7 14.0 %copy-start = (f32[128,1536]{1,0:T(8,128)S(1)}, f32[128,1536]{1,0:T(8,128)}, u32[]{:S(2)}) copy-start(f32[128,1536]{1,0:T(8,128)} %get-tuple-element.103) | copy-start | bytes 2359300
